TPU v7x, 32 devices: a whole 2x2x4 slice. The times are simulated.
32 devices in a mesh: section: 2 (over y), dp: 4 (over z), tensor: 4 (over x, core).
Axes of the slice: x: 2, y: 2, z: 4, core: 2. Of those that a mesh axis runs over, the one named last changes fastest.
Arguments:
- text_input: bfloat16 [2, 8, 512, 768], P('section', 'dp', 'tensor'), may hold values from -6 to 6
- layout_input: bfloat16 [2, 8, 512, 192], P('section', 'dp', 'tensor'), may hold values from -6 to 6
- text_cotangent: bfloat16 [2, 8, 512, 768], P('section', 'dp', 'tensor'), may hold values from -6 to 6
- layout_cotangent: bfloat16 [2, 8, 512, 192], P('section', 'dp', 'tensor'), may hold values from -6 to 6
- page_counts: int32 [2, 8], P(None, 'dp'), may hold values from 64 to 512, as said below
- pad_mask: int32 [2, 8, 512], P(None, 'dp'), may hold values 0 or 1
- lang_ids: int32 [2, 8], P(None, 'dp'), may hold values from 0 to 7
- lang_table: float32 [8, 768], replicated, may hold values from -3 to 3
- text_project: bfloat16 [2, 768, 3, 768], P('section', None, None, 'tensor'), may hold values from -0.21875 to 0.21875
- text_outward: bfloat16 [2, 768, 768], P('section', 'tensor'), may hold values from -0.875 to 0.875
- text_upward: bfloat16 [2, 768, 3072], P('section', None, 'tensor'), may hold values from -0.21875 to 0.21875
- text_downward: bfloat16 [2, 3072, 768], P('section', 'tensor'), may hold values from -0.109375 to 0.109375
- text_gains: float32 [2, 2, 768], P('section'), may hold values from 0.25 to 1.75
- text_biases: float32 [2, 2, 768], P('section'), may hold values from -1.8 to 1.8
- layout_project: bfloat16 [2, 192, 3, 192], P('section', None, None, 'tensor'), may hold values from -0.4375 to 0.4375
- layout_outward: bfloat16 [2, 192, 192], P('section', 'tensor'), may hold values from -1.75 to 1.75
- layout_upward: bfloat16 [2, 192, 768], P('section', None, 'tensor'), may hold values from -0.4375 to 0.4375
- layout_downward: bfloat16 [2, 768, 192], P('section', 'tensor'), may hold values from -0.21875 to 0.21875
- layout_gains: float32 [2, 2, 192], P('section'), may hold values from 0.25 to 1.75
- layout_biases: float32 [2, 2, 192], P('section'), may hold values from -1.8 to 1.8
Outputs:
- text_output: bfloat16 [2, 8, 512, 768], P('section', 'dp', 'tensor')
- layout_output: bfloat16 [2, 8, 512, 192], P('section', 'dp', 'tensor')
- text_input_gradient: bfloat16 [2, 8, 512, 768], P('section', 'dp', 'tensor')
- layout_input_gradient: bfloat16 [2, 8, 512, 192], P('section', 'dp', 'tensor')
- lang_table_gradient: float32 [8, 768], replicated
- text_project_gradient: float32 [2, 768, 3, 768], P('section', None, None, 'tensor')
- text_outward_gradient: float32 [2, 768, 768], P('section', 'tensor')
- text_upward_gradient: float32 [2, 768, 3072], P('section', None, 'tensor')
- text_downward_gradient: float32 [2, 3072, 768], P('section', 'tensor')
- text_gains_gradient: float32 [2, 2, 768], P('section')
- text_biases_gradient: float32 [2, 2, 768], P('section')
- layout_project_gradient: float32 [2, 192, 3, 192], P('section', None, None, 'tensor')
- layout_outward_gradient: float32 [2, 192, 192], P('section', 'tensor')
- layout_upward_gradient: float32 [2, 192, 768], P('section', None, 'tensor')
- layout_downward_gradient: float32 [2, 768, 192], P('section', 'tensor')
- layout_gains_gradient: float32 [2, 2, 192], P('section')
- layout_biases_gradient: float32 [2, 2, 192], P('section')
Inputs may be any that keep to these rules, and one draw needn't show every extreme that they name: `page_counts`: in every draw one page holds all 512 tokens; position 0 of a page always counts as a key.
All inputs are finite; a program needn't handle non-finite values. No bound on the sum of `pad_mask` on one device may be relied on, other than what follows from the above.
Results may differ from a plain program's by a relative error of at most 0.035.
Values may be sent and summed in bfloat16 or wider, within the bound.
A program may use at most 192 MiB of HBM per device.

v0:
```python
import math

import jax
import jax.numpy as jnp
from jax import lax
from jax.sharding import PartitionSpec as P

HEAD_TEXT = 64
HEAD_LAYOUT = 16


EPSILON = 1e-05
NEGATIVE = -1e30
HIGH = lax.Precision.HIGHEST


def shifted(block, axis, distance):
    devices = range(lax.axis_size(axis))
    route = [(i - distance, i) for i in devices if i - distance in devices]
    return lax.ppermute(block, axis, route)


def from_behind(block, axis, distance):
    devices = range(lax.axis_size(axis))
    route = [((i - distance) % len(devices), i) for i in devices]
    return lax.ppermute(block, axis, route)


def gather_rows(text_part, layout_part):
    return (
        lax.all_gather(text_part, "tensor", axis=1, tiled=True),
        lax.all_gather(layout_part, "tensor", axis=1, tiled=True),
    )


def sum_rows(text_part, layout_part):
    return (
        lax.psum_scatter(
            text_part.astype(jnp.bfloat16), "tensor", scatter_dimension=1, tiled=True
        ).astype(jnp.float32),
        lax.psum_scatter(
            layout_part.astype(jnp.bfloat16), "tensor", scatter_dimension=1, tiled=True
        ).astype(jnp.float32),
    )


def gather_grads(text_part, layout_part):
    return (
        lax.all_gather(text_part, "tensor", axis=1, tiled=True),
        lax.all_gather(layout_part, "tensor", axis=1, tiled=True),
    )


def sum_grads(text_part, layout_part):
    return (
        lax.psum_scatter(
            text_part.astype(jnp.bfloat16), "tensor", scatter_dimension=1, tiled=True
        ).astype(jnp.float32),
        lax.psum_scatter(
            layout_part.astype(jnp.bfloat16), "tensor", scatter_dimension=1, tiled=True
        ).astype(jnp.float32),
    )


def norm_forward(summed, gain, offset):
    center = summed - jnp.mean(summed, axis=-1, keepdims=True)
    inverse = lax.rsqrt(jnp.mean(center * center, axis=-1, keepdims=True) + EPSILON)
    normed = center * inverse
    return (normed * gain + offset, normed, inverse)


def norm_backward(upstream, normed, inverse, gain):
    scaled = upstream * gain
    mean_scaled = jnp.mean(scaled, axis=-1, keepdims=True)
    mean_product = jnp.mean(scaled * normed, axis=-1, keepdims=True)
    downstream = inverse * (scaled - mean_scaled - normed * mean_product)
    return (downstream, jnp.sum(upstream * normed, axis=(0, 1)), jnp.sum(upstream, axis=(0, 1)))


def activation(values):
    return jax.nn.gelu(values, approximate=False)


def activation_backward(values, upstream):
    unused, pullback = jax.vjp(activation, values)
    return pullback(upstream)[0]


def stream_heads(full_rows, project, head_size):
    projected = jnp.einsum(
        "pld,dn->pln", full_rows, project, preferred_element_type=jnp.float32
    ).astype(jnp.bfloat16)
    return projected.reshape(projected.shape[0], projected.shape[1], 3, -1, head_size)


def joint_scores(heads_pair, key_valid):
    text_set, layout_set = heads_pair
    scores = jnp.einsum(
        "pqhd,pkhd->phqk", text_set[:, :, 0], text_set[:, :, 1], preferred_element_type=jnp.float32
    ) * (1.0 / math.sqrt(HEAD_TEXT))
    scores = scores + jnp.einsum(
        "pqhd,pkhd->phqk",
        layout_set[:, :, 0],
        layout_set[:, :, 1],
        preferred_element_type=jnp.float32,
    ) * (1.0 / math.sqrt(HEAD_LAYOUT))
    return jnp.where(key_valid[:, None, None, :], scores, NEGATIVE)


def layer_forward(rows_pair, streams, key_valid):
    full_pair = gather_rows(rows_pair[0], rows_pair[1])
    heads_pair = (
        stream_heads(full_pair[0], streams[0][0], HEAD_TEXT),
        stream_heads(full_pair[1], streams[1][0], HEAD_LAYOUT),
    )
    scores = joint_scores(heads_pair, key_valid)
    highest = jnp.max(scores, axis=-1, keepdims=True)
    log_total = jnp.log(jnp.sum(jnp.exp(scores - highest), axis=-1, keepdims=True)) + highest
    probs = jnp.exp(scores - log_total).astype(jnp.bfloat16)
    contexts = []
    partials = []
    for branch in range(2):
        context = jnp.einsum(
            "phqk,pkhd->pqhd",
            probs,
            heads_pair[branch][:, :, 2],
            preferred_element_type=jnp.float32,
        ).astype(jnp.bfloat16)
        context = context.reshape(context.shape[0], context.shape[1], -1)
        contexts.append(context)
        partials.append(
            jnp.einsum(
                "pln,nd->pld", context, streams[branch][1], preferred_element_type=jnp.float32
            )
        )
    attended = sum_rows(partials[0], partials[1])
    hiddens = []
    normed_one = []
    inverse_one = []
    for branch in range(2):
        hidden, normed, inverse = norm_forward(
            rows_pair[branch].astype(jnp.float32) + attended[branch],
            streams[branch][4][0],
            streams[branch][5][0],
        )
        hiddens.append(hidden)
        normed_one.append(normed)
        inverse_one.append(inverse)
    hidden_full = gather_rows(hiddens[0].astype(jnp.bfloat16), hiddens[1].astype(jnp.bfloat16))
    pre_list = []
    active_list = []
    fed_parts = []
    for branch in range(2):
        pre_act = jnp.einsum(
            "pld,dn->pln",
            hidden_full[branch],
            streams[branch][2],
            preferred_element_type=jnp.float32,
        )
        active = activation(pre_act).astype(jnp.bfloat16)
        pre_list.append(pre_act)
        active_list.append(active)
        fed_parts.append(
            jnp.einsum(
                "pln,nd->pld", active, streams[branch][3], preferred_element_type=jnp.float32
            )
        )
    fed = sum_rows(fed_parts[0], fed_parts[1])
    outputs = []
    normed_two = []
    inverse_two = []
    for branch in range(2):
        output, normed, inverse = norm_forward(
            hiddens[branch] + fed[branch], streams[branch][4][1], streams[branch][5][1]
        )
        outputs.append(output)
        normed_two.append(normed)
        inverse_two.append(inverse)
    saved = {
        "full_pair": full_pair,
        "heads_pair": heads_pair,
        "log_total": log_total,
        "contexts": contexts,
        "normed_one": normed_one,
        "inverse_one": inverse_one,
        "hidden_full": hidden_full,
        "pre_list": pre_list,
        "active_list": active_list,
        "normed_two": normed_two,
        "inverse_two": inverse_two,
    }
    return ((outputs[0], outputs[1]), saved)


def layer_backward(saved, grads_pair, streams, key_valid):
    weight_grads = [[None] * 4, [None] * 4]
    gain_grads = [[None, None], [None, None]]
    bias_grads = [[None, None], [None, None]]
    dz_two = []
    for branch in range(2):
        downstream, gain_part, bias_part = norm_backward(
            grads_pair[branch],
            saved["normed_two"][branch],
            saved["inverse_two"][branch],
            streams[branch][4][1],
        )
        dz_two.append(downstream)
        gain_grads[branch][1] = gain_part
        bias_grads[branch][1] = bias_part
    upstream = gather_grads(dz_two[0].astype(jnp.bfloat16), dz_two[1].astype(jnp.bfloat16))
    back_parts = []
    for branch in range(2):
        weight_grads[branch][3] = jnp.einsum(
            "pln,pld->nd",
            saved["active_list"][branch],
            upstream[branch],
            preferred_element_type=jnp.float32,
        )
        active_grad = jnp.einsum(
            "pld,nd->pln", upstream[branch], streams[branch][3], preferred_element_type=jnp.float32
        )
        pre_grad = activation_backward(saved["pre_list"][branch], active_grad).astype(jnp.bfloat16)
        weight_grads[branch][2] = jnp.einsum(
            "pld,pln->dn",
            saved["hidden_full"][branch],
            pre_grad,
            preferred_element_type=jnp.float32,
        )
        back_parts.append(
            jnp.einsum(
                "pln,dn->pld", pre_grad, streams[branch][2], preferred_element_type=jnp.float32
            )
        )
    backed = sum_grads(back_parts[0], back_parts[1])
    dz_one = []
    for branch in range(2):
        downstream, gain_part, bias_part = norm_backward(
            dz_two[branch] + backed[branch],
            saved["normed_one"][branch],
            saved["inverse_one"][branch],
            streams[branch][4][0],
        )
        dz_one.append(downstream)
        gain_grads[branch][0] = gain_part
        bias_grads[branch][0] = bias_part
    upstream = gather_grads(dz_one[0].astype(jnp.bfloat16), dz_one[1].astype(jnp.bfloat16))
    heads_pair = saved["heads_pair"]
    context_grads = []
    for branch in range(2):
        weight_grads[branch][1] = jnp.einsum(
            "pln,pld->nd",
            saved["contexts"][branch],
            upstream[branch],
            preferred_element_type=jnp.float32,
        )
        context_grad = jnp.einsum(
            "pld,nd->pln", upstream[branch], streams[branch][1], preferred_element_type=jnp.float32
        ).astype(jnp.bfloat16)
        context_grads.append(context_grad.reshape(heads_pair[branch][:, :, 2].shape))
    scores = joint_scores(heads_pair, key_valid)
    probs = jnp.exp(scores - saved["log_total"])
    probs_low = probs.astype(jnp.bfloat16)
    scores_grads = []
    for branch in range(2):
        probs_grad = jnp.einsum(
            "pqhd,pkhd->phqk",
            context_grads[branch],
            heads_pair[branch][:, :, 2],
            preferred_element_type=jnp.float32,
        )
        inner_sum = jnp.sum(probs * probs_grad, axis=-1, keepdims=True)
        scores_grads.append((probs * (probs_grad - inner_sum)).astype(jnp.bfloat16))
    scales = (1.0 / math.sqrt(HEAD_TEXT), 1.0 / math.sqrt(HEAD_LAYOUT))
    back_parts = []
    for branch in range(2):
        head_set = heads_pair[branch]
        reaching = [scores_grads[1]] if branch == 1 else [scores_grads[0], scores_grads[1]]
        query_sum = None
        key_sum = None
        for grad_block in reaching:
            query_part = jnp.einsum(
                "phqk,pkhd->pqhd", grad_block, head_set[:, :, 1], preferred_element_type=jnp.float32
            )
            key_part = jnp.einsum(
                "phqk,pqhd->pkhd", grad_block, head_set[:, :, 0], preferred_element_type=jnp.float32
            )
            query_sum = query_part if query_sum is None else query_sum + query_part
            key_sum = key_part if key_sum is None else key_sum + key_part
        query_grad = (query_sum * scales[branch]).astype(jnp.bfloat16)
        key_grad = (key_sum * scales[branch]).astype(jnp.bfloat16)
        value_grad = jnp.einsum(
            "phqk,pqhd->pkhd", probs_low, context_grads[branch], preferred_element_type=jnp.float32
        ).astype(jnp.bfloat16)
        stacked = jnp.stack([query_grad, key_grad, value_grad], axis=2)
        stacked = stacked.reshape(stacked.shape[0], stacked.shape[1], -1)
        weight_grads[branch][0] = jnp.einsum(
            "pld,pln->dn", saved["full_pair"][branch], stacked, preferred_element_type=jnp.float32
        )
        back_parts.append(
            jnp.einsum(
                "pln,dn->pld", stacked, streams[branch][0], preferred_element_type=jnp.float32
            )
        )
    backed = sum_grads(back_parts[0], back_parts[1])
    input_grads = (dz_one[0] + backed[0], dz_one[1] + backed[1])
    flat_weights = tuple(weight_grads[0]) + tuple(weight_grads[1])
    norm_grads = (
        jnp.stack(gain_grads[0]),
        jnp.stack(bias_grads[0]),
        jnp.stack(gain_grads[1]),
        jnp.stack(bias_grads[1]),
    )
    return (input_grads, flat_weights, norm_grads)


def per_device(
    text_input,
    layout_input,
    text_cotangent,
    layout_cotangent,
    page_counts,
    pad_mask,
    lang_ids,
    lang_table,
    text_project,
    text_outward,
    text_upward,
    text_downward,
    text_gains,
    text_biases,
    layout_project,
    layout_outward,
    layout_upward,
    layout_downward,
    layout_gains,
    layout_biases,
):
    section_index = lax.axis_index("section")
    streams = (
        (
            text_project[0].reshape(text_project.shape[1], -1),
            text_outward[0],
            text_upward[0],
            text_downward[0],
            text_gains[0],
            text_biases[0],
        ),
        (
            layout_project[0].reshape(layout_project.shape[1], -1),
            layout_outward[0],
            layout_upward[0],
            layout_downward[0],
            layout_gains[0],
            layout_biases[0],
        ),
    )
    own_ids = lax.dynamic_index_in_dim(lang_ids, section_index, 0, keepdims=False)
    lang_onehot = (
        own_ids[:, None] == jnp.arange(lang_table.shape[0], dtype=jnp.int32)[None, :]
    ).astype(jnp.float32)
    lang_rows = jnp.dot(lang_onehot, lang_table, precision=HIGH)
    embedded = (text_input[0].astype(jnp.float32) + lang_rows[:, None, :]).astype(jnp.bfloat16)
    own_layout = layout_input[0]
    late_text, late_layout = shifted((embedded, own_layout), "section", -1)

    def valid_for(micro_index):
        counts_row = lax.dynamic_index_in_dim(page_counts, micro_index, 0, keepdims=False)
        mask_row = lax.dynamic_index_in_dim(pad_mask, micro_index, 0, keepdims=False)
        positions = jnp.arange(mask_row.shape[1], dtype=jnp.int32)
        return (positions[None, :] < counts_row[:, None]) & (
            (mask_row == 1) | (positions[None, :] == 0)
        )

    current = (embedded, own_layout)
    inputs = []
    stores = []
    for moment in range(3):
        if moment == 1:
            current = (
                jnp.where(section_index == 0, late_text, current[0]),
                jnp.where(section_index == 0, late_layout, current[1]),
            )
        micro_index = jnp.clip(moment - section_index, 0, 1)
        outputs, saved = layer_forward(current, streams, valid_for(micro_index))
        inputs.append(current)
        stores.append(saved)
        rounded = (outputs[0].astype(jnp.bfloat16), outputs[1].astype(jnp.bfloat16))
        if moment < 2:
            current = from_behind((rounded[0], rounded[1]), "section", 1)
        else:
            final_text = jnp.where(section_index == 0, current[0], rounded[0])
            final_layout = jnp.where(section_index == 0, current[1], rounded[1])
    own_cotangent = (text_cotangent[0], layout_cotangent[0])
    late_cot_text, late_cot_layout = shifted((own_cotangent[0], own_cotangent[1]), "section", 1)
    incoming = own_cotangent
    weight_totals = None
    norm_totals = None
    for moment in range(3):
        forward_moment = 2 - moment
        if moment == 1:
            incoming = (
                jnp.where(section_index == 1, late_cot_text, incoming[0]),
                jnp.where(section_index == 1, late_cot_layout, incoming[1]),
            )
        micro_index = jnp.clip(forward_moment - section_index, 0, 1)
        key_valid = valid_for(micro_index)
        unused, saved = layer_forward(inputs[forward_moment], streams, key_valid)
        input_grads, weight_grads, norm_grads = layer_backward(
            saved,
            (incoming[0].astype(jnp.float32), incoming[1].astype(jnp.float32)),
            streams,
            key_valid,
        )
        active_turn = (moment >= 1 - section_index) & (moment <= 2 - section_index)
        masked_weights = tuple((jnp.where(active_turn, member, 0.0) for member in weight_grads))
        masked_norms = tuple((jnp.where(active_turn, member, 0.0) for member in norm_grads))
        if weight_totals is None:
            weight_totals = masked_weights
            norm_totals = masked_norms
        else:
            weight_totals = tuple(
                (total + member for total, member in zip(weight_totals, masked_weights))
            )
            norm_totals = tuple(
                (total + member for total, member in zip(norm_totals, masked_norms))
            )
        rounded_grads = (input_grads[0].astype(jnp.bfloat16), input_grads[1].astype(jnp.bfloat16))
        if moment < 2:
            incoming = from_behind((rounded_grads[0], rounded_grads[1]), "section", -1)
        else:
            text_grad_final = jnp.where(section_index == 0, rounded_grads[0], incoming[0])
            layout_grad_final = jnp.where(section_index == 0, rounded_grads[1], incoming[1])
    page_sums = jnp.sum(text_grad_final.astype(jnp.float32), axis=1)
    lang_grad = jnp.dot(lang_onehot.T, page_sums, precision=HIGH)
    section_pick = (jnp.arange(2, dtype=jnp.int32) == section_index).astype(jnp.float32)[
        :, None, None
    ]
    summed_small = lax.psum(
        (
            section_pick * norm_totals[0][None],
            section_pick * norm_totals[1][None],
            section_pick * norm_totals[2][None],
            section_pick * norm_totals[3][None],
            lang_grad,
        ),
        ("section", "dp", "tensor"),
    )
    summed_weights = (
        lax.psum(weight_totals[0].astype(jnp.bfloat16), "dp").astype(jnp.float32),
        lax.psum(weight_totals[1].astype(jnp.bfloat16), "dp").astype(jnp.float32),
        lax.psum(weight_totals[2].astype(jnp.bfloat16), "dp").astype(jnp.float32),
        lax.psum(weight_totals[3].astype(jnp.bfloat16), "dp").astype(jnp.float32),
        lax.psum(weight_totals[4].astype(jnp.bfloat16), "dp").astype(jnp.float32),
        lax.psum(weight_totals[5].astype(jnp.bfloat16), "dp").astype(jnp.float32),
        lax.psum(weight_totals[6].astype(jnp.bfloat16), "dp").astype(jnp.float32),
        lax.psum(weight_totals[7].astype(jnp.bfloat16), "dp").astype(jnp.float32),
    )

    def own_row(stacked):
        return lax.dynamic_slice_in_dim(stacked, section_index, 1, 0)

    return (
        final_text[None],
        final_layout[None],
        text_grad_final[None],
        layout_grad_final[None],
        summed_small[4],
        summed_weights[0].reshape(text_project.shape),
        summed_weights[1][None],
        summed_weights[2][None],
        summed_weights[3][None],
        own_row(summed_small[0]),
        own_row(summed_small[1]),
        summed_weights[4].reshape(layout_project.shape),
        summed_weights[5][None],
        summed_weights[6][None],
        summed_weights[7][None],
        own_row(summed_small[2]),
        own_row(summed_small[3]),
    )


def solution(mesh):
    in_specs = (
        P("section", "dp", "tensor", None),
        P("section", "dp", "tensor", None),
        P("section", "dp", "tensor", None),
        P("section", "dp", "tensor", None),
        P(None, "dp"),
        P(None, "dp", None),
        P(None, "dp"),
        P(),
        P("section", None, None, "tensor"),
        P("section", "tensor", None),
        P("section", None, "tensor"),
        P("section", "tensor", None),
        P("section", None, None),
        P("section", None, None),
        P("section", None, None, "tensor"),
        P("section", "tensor", None),
        P("section", None, "tensor"),
        P("section", "tensor", None),
        P("section", None, None),
        P("section", None, None),
    )
    out_specs = (
        P("section", "dp", "tensor", None),
        P("section", "dp", "tensor", None),
        P("section", "dp", "tensor", None),
        P("section", "dp", "tensor", None),
        P(),
        P("section", None, None, "tensor"),
        P("section", "tensor", None),
        P("section", None, "tensor"),
        P("section", "tensor", None),
        P("section", None, None),
        P("section", None, None),
        P("section", None, None, "tensor"),
        P("section", "tensor", None),
        P("section", None, "tensor"),
        P("section", "tensor", None),
        P("section", None, None),
        P("section", None, None),
    )
    return jax.shard_map(
        per_device, mesh=mesh, in_specs=in_specs, out_specs=out_specs, check_vma=False
    )
```

profile of v0, /device:TPU:0, one launch (start us, length us, event | category | flops | bytes accessed | tf_op | source)
XLA Modules:
  0.0 1265.4 jit_solution(12769867598262971813)
XLA Ops:
  23.0 10.9 all-gather.14.cloned.1.call-done
  48.3 28.2 %reduce-scatter.49.cloned.1.call-done = bf16[2,128,768]{2,1,0:T(8,128)(2,1)} async-done(((bf16[2,512,768]{2,1,0:T(8,128)(2,1)}), bf16[2,128,768]{2,1,0:T(8,128)(2,1)}) %reduce-scatter.49.cloned.1.call-update) | async-done | bytes 393232 | tf_op jit(solution)/shard_map/reduce_scatter | solution.py:38
  85.5 15.3 %all-gather.16.cloned.1.call-done = bf16[2,512,768]{2,1,0:T(8,128)(2,1)} async-done(((bf16[2,128,768]{2,1,0:T(8,128)(2,1)}), bf16[2,512,768]{2,1,0:T(8,128)(2,1)}) %all-gather.16.cloned.1.call-update) | async-done | bytes 1572880 | tf_op jit(solution)/shard_map/all_gather | solution.py:31
  140.6 15.5 %reduce-scatter.51.cloned.1.call-done = bf16[2,128,768]{2,1,0:T(8,128)(2,1)} async-done(((bf16[2,512,768]{2,1,0:T(8,128)(2,1)}), bf16[2,128,768]{2,1,0:T(8,128)(2,1)}) %reduce-scatter.51.cloned.1.call-update) | async-done | bytes 393232 | tf_op jit(solution)/shard_map/reduce_scatter | solution.py:38
  215.4 28.5 %reduce-scatter.53.cloned.1.call-done = bf16[2,128,768]{2,1,0:T(8,128)(2,1)} async-done(((bf16[2,512,768]{2,1,0:T(8,128)(2,1)}), bf16[2,128,768]{2,1,0:T(8,128)(2,1)}) %reduce-scatter.53.cloned.1.call-update) | async-done | bytes 393232 | tf_op jit(solution)/shard_map/reduce_scatter | solution.py:38
  253.1 15.1 %all-gather.20.cloned.1.call-done = bf16[2,512,768]{2,1,0:T(8,128)(2,1)} async-done(((bf16[2,128,768]{2,1,0:T(8,128)(2,1)}), bf16[2,512,768]{2,1,0:T(8,128)(2,1)}) %all-gather.20.cloned.1.call-update) | async-done | bytes 1572880 | tf_op jit(solution)/shard_map/all_gather | solution.py:31
  307.2 16.4 %reduce-scatter.55.cloned.1.call-done = bf16[2,128,768]{2,1,0:T(8,128)(2,1)} async-done(((bf16[2,512,768]{2,1,0:T(8,128)(2,1)}), bf16[2,128,768]{2,1,0:T(8,128)(2,1)}) %reduce-scatter.55.cloned.1.call-update) | async-done | bytes 393232 | tf_op jit(solution)/shard_map/reduce_scatter | solution.py:38
  383.6 28.6 %reduce-scatter.57.cloned.1.call-done = bf16[2,128,768]{2,1,0:T(8,128)(2,1)} async-done(((bf16[2,512,768]{2,1,0:T(8,128)(2,1)}), bf16[2,128,768]{2,1,0:T(8,128)(2,1)}) %reduce-scatter.57.cloned.1.call-update) | async-done | bytes 393232 | tf_op jit(solution)/shard_map/reduce_scatter | solution.py:38
  416.7 19.8 %all-gather.24.cloned.1.call-done = bf16[2,512,768]{2,1,0:T(8,128)(2,1)} async-done(((bf16[2,128,768]{2,1,0:T(8,128)(2,1)}), bf16[2,512,768]{2,1,0:T(8,128)(2,1)}) %all-gather.24.cloned.1.call-update) | async-done | bytes 1572880 | tf_op jit(solution)/shard_map/all_gather | solution.py:31
  457.9 22.1 %reduce-scatter.59.cloned.1.call-done = bf16[2,128,768]{2,1,0:T(8,128)(2,1)} async-done(((bf16[2,512,768]{2,1,0:T(8,128)(2,1)}), bf16[2,128,768]{2,1,0:T(8,128)(2,1)}) %reduce-scatter.59.cloned.1.call-update) | async-done | bytes 393232 | tf_op jit(solution)/shard_map/reduce_scatter | solution.py:38
  483.8 20.0 %reduce-scatter.81.cloned.1.call-done = bf16[128,384]{1,0:T(8,128)(2,1)} async-done(((bf16[512,384]{1,0:T(8,128)(2,1)}), bf16[128,384]{1,0:T(8,128)(2,1)}) %reduce-scatter.81.cloned.1.call-update) | async-done | bytes 98320
  535.0 13.9 %reduce-scatter.83.cloned.1.call-done = bf16[128,384]{1,0:T(8,128)(2,1)} async-done(((bf16[512,384]{1,0:T(8,128)(2,1)}), bf16[128,384]{1,0:T(8,128)(2,1)}) %reduce-scatter.83.cloned.1.call-update) | async-done | bytes 98320
  569.2 10.8 reduce-scatter.61.cloned.1.call-done
  584.9 18.6 %reduce-scatter.85.cloned.1.call-done = bf16[128,384]{1,0:T(8,128)(2,1)} async-done(((bf16[512,384]{1,0:T(8,128)(2,1)}), bf16[128,384]{1,0:T(8,128)(2,1)}) %reduce-scatter.85.cloned.1.call-update) | async-done | bytes 98320
  649.9 24.0 %reduce-scatter.63.cloned.1.call-done = bf16[2,128,768]{2,1,0:T(8,128)(2,1)} async-done(((bf16[2,512,768]{2,1,0:T(8,128)(2,1)}), bf16[2,128,768]{2,1,0:T(8,128)(2,1)}) %reduce-scatter.63.cloned.1.call-update) | async-done | bytes 393232 | tf_op jit(solution)/shard_map/reduce_scatter | solution.py:56
  696.2 14.2 %all-gather.30.cloned.1.call-done = bf16[2,512,768]{2,1,0:T(8,128)(2,1)} async-done(((bf16[2,128,768]{2,1,0:T(8,128)(2,1)}), bf16[2,512,768]{2,1,0:T(8,128)(2,1)}) %all-gather.30.cloned.1.call-update) | async-done | bytes 1572880 | tf_op jit(solution)/shard_map/all_gather | solution.py:49
  723.3 10.4 reduce-scatter.87.cloned.1.call-done
  769.4 18.8 %reduce-scatter.89.cloned.1.call-done = bf16[128,384]{1,0:T(8,128)(2,1)} async-done(((bf16[512,384]{1,0:T(8,128)(2,1)}), bf16[128,384]{1,0:T(8,128)(2,1)}) %reduce-scatter.89.cloned.1.call-update) | async-done | bytes 98320
  830.4 28.3 %reduce-scatter.67.cloned.1.call-done = bf16[2,128,768]{2,1,0:T(8,128)(2,1)} async-done(((bf16[2,512,768]{2,1,0:T(8,128)(2,1)}), bf16[2,128,768]{2,1,0:T(8,128)(2,1)}) %reduce-scatter.67.cloned.1.call-update) | async-done | bytes 393232 | tf_op jit(solution)/shard_map/reduce_scatter | solution.py:56
  959.6 11.5 reduce-scatter.93.cloned.1.call-done
  1056.3 13.8 %reduce-scatter.95.cloned.1.call-done = bf16[128,384]{1,0:T(8,128)(2,1)} async-done(((bf16[512,384]{1,0:T(8,128)(2,1)}), bf16[128,384]{1,0:T(8,128)(2,1)}) %reduce-scatter.95.cloned.1.call-update) | async-done | bytes 98320
  1072.9 27.7 %reduce-scatter.71.cloned.1.call-done = bf16[2,128,768]{2,1,0:T(8,128)(2,1)} async-done(((bf16[2,512,768]{2,1,0:T(8,128)(2,1)}), bf16[2,128,768]{2,1,0:T(8,128)(2,1)}) %reduce-scatter.71.cloned.1.call-update) | async-done | bytes 393232 | tf_op jit(solution)/shard_map/reduce_scatter | solution.py:56
  1104.0 46.6 %all-reduce = (f32[8,768]{1,0:T(8,128)}, f32[2,2,768]{2,1,0:T(2,128)S(1)}, f32[2,2,768]{2,1,0:T(2,128)S(1)}, f32[2,2,192]{2,1,0:T(2,128)S(1)}, f32[2,2,192]{2,1,0:T(2,128)S(1)}) all-reduce(f32[8,768]{1,0:T(8,128)S(1)} %fusion.286, ...), channel_id=1, replica_groups=mesh['section'=2,'dp'=4,'tensor'=4] {'section','dp','tensor'}, use_global_device_ids=true, to_apply=%region_85.86 | all-reduce | flops 13824 | bytes 110592 | tf_op jit(solution)/shard_map/psum | solution.py:438
  1151.8 96.0 %all-reduce.8.cloned.1.call-done = (bf16[1,768,3,192]{1,3,2,0:T(8,128)(2,1)}, bf16[1,192,768]{2,1,0:T(8,128)(2,1)}, bf16[1,768,768]{2,1,0:T(8,128)(2,1)}, bf16[1...) async-done(((bf16[1,768,3,192]{1,3,2,0:T(8,128)(2,1)}, bf16[1,192,768]{2,1,0:T(8,128)(2,1)}, bf16[1,768,768]{2,1,0:T(8,128)(2,1)}, ...) | async-done | bytes 3686416 | tf_op jit(solution)/shard_map/psum | solution.py:449
  (1174 shorter events, 691.8 us)
Async XLA Ops:
  11.3 65.2 %reduce-scatter.49.cloned.1.call-start = ((), (), s32[]{:S(2)}) async-start(), calls=%async_computation.25 | async-start | bytes 1966080 | tf_op jit(solution)/shard_map/reduce_scatter | solution.py:38
  85.3 70.8 %reduce-scatter.51.cloned.1.call-start = ((), (), s32[]{:S(2)}) async-start(), calls=%async_computation.27 | async-start | bytes 1966080 | tf_op jit(solution)/shard_map/reduce_scatter | solution.py:38
  116.3 63.6 %reduce-scatter.75.cloned.1.call-start = ((), (), s32[]{:S(2)}) async-start(), calls=%async_computation.49 | async-start | bytes 491520
  140.5 61.2 %all-gather.18.cloned.1.call-start = ((), (), s32[]{:S(2)}) async-start(), calls=%async_computation.28 | async-start | bytes 1966080 | tf_op jit(solution)/shard_map/all_gather | solution.py:31
  171.3 72.6 %reduce-scatter.53.cloned.1.call-start = ((), (), s32[]{:S(2)}) async-start(), calls=%async_computation.29 | async-start | bytes 1966080 | tf_op jit(solution)/shard_map/reduce_scatter | solution.py:38
  252.7 70.9 %reduce-scatter.55.cloned.1.call-start = ((), (), s32[]{:S(2)}) async-start(), calls=%async_computation.31 | async-start | bytes 1966080 | tf_op jit(solution)/shard_map/reduce_scatter | solution.py:38
  283.6 63.7 %reduce-scatter.79.cloned.1.call-start = ((), (), s32[]{:S(2)}) async-start(), calls=%async_computation.51 | async-start | bytes 491520
  307.1 62.9 %all-gather.22.cloned.1.call-start = ((), (), s32[]{:S(2)}) async-start(), calls=%async_computation.32 | async-start | bytes 1966080 | tf_op jit(solution)/shard_map/all_gather | solution.py:31
  337.5 74.7 %reduce-scatter.57.cloned.1.call-start = ((), (), s32[]{:S(2)}) async-start(), calls=%async_computation.33 | async-start | bytes 1966080 | tf_op jit(solution)/shard_map/reduce_scatter | solution.py:38
  416.6 63.4 %reduce-scatter.59.cloned.1.call-start = ((), (), s32[]{:S(2)}) async-start(), calls=%async_computation.35 | async-start | bytes 1966080 | tf_op jit(solution)/shard_map/reduce_scatter | solution.py:38
  457.9 67.6 %all-gather.26.cloned.1.call-start = ((), (), s32[]{:S(2)}) async-start(), calls=%async_computation.36 | async-start | bytes 1966080 | tf_op jit(solution)/shard_map/all_gather | solution.py:49
  483.7 65.1 %reduce-scatter.83.cloned.1.call-start = ((), (), s32[]{:S(2)}) async-start(), calls=%async_computation.53 | async-start | bytes 491520
  534.9 68.6 %reduce-scatter.85.cloned.1.call-start = ((), (), s32[]{:S(2)}) async-start(), calls=%async_computation.54 | async-start | bytes 491520
  584.5 89.5 %reduce-scatter.63.cloned.1.call-start = ((), (), s32[]{:S(2)}) async-start(), calls=%async_computation.39 | async-start | bytes 1966080 | tf_op jit(solution)/shard_map/reduce_scatter | solution.py:56
  645.6 64.7 %all-gather.30.cloned.1.call-start = ((), (), s32[]{:S(2)}) async-start(), calls=%async_computation.40 | async-start | bytes 1966080 | tf_op jit(solution)/shard_map/all_gather | solution.py:49
  696.0 68.9 %reduce-scatter.65.cloned.1.call-start = ((), (), s32[]{:S(2)}) async-start(), calls=%async_computation.41 | async-start | bytes 1966080 | tf_op jit(solution)/shard_map/reduce_scatter | solution.py:56
  719.8 68.4 %reduce-scatter.89.cloned.1.call-start = ((), (), s32[]{:S(2)}) async-start(), calls=%async_computation.56 | async-start | bytes 491520
  769.3 89.3 %reduce-scatter.67.cloned.1.call-start = ((), (), s32[]{:S(2)}) async-start(), calls=%async_computation.43 | async-start | bytes 1966080 | tf_op jit(solution)/shard_map/reduce_scatter | solution.py:56
  830.3 62.7 %all-gather.34.cloned.1.call-start = ((), (), s32[]{:S(2)}) async-start(), calls=%async_computation.44 | async-start | bytes 1966080 | tf_op jit(solution)/shard_map/all_gather | solution.py:49
  887.7 60.0 %reduce-scatter.69.cloned.1.call-start = ((), (), s32[]{:S(2)}) async-start(), calls=%async_computation.45 | async-start | bytes 1966080 | tf_op jit(solution)/shard_map/reduce_scatter | solution.py:56
  902.5 68.5 %reduce-scatter.93.cloned.1.call-start = ((), (), s32[]{:S(2)}) async-start(), calls=%async_computation.58 | async-start | bytes 491520
  952.3 101.1 %all-reduce.6.cloned.1.call-start = ((), (), s32[]{:S(2)}) async-start(), calls=%async_computation.60 | async-start | bytes 196608 | tf_op jit(solution)/shard_map/psum | solution.py:453
  1019.0 81.7 %reduce-scatter.71.cloned.1.call-start = ((), (), s32[]{:S(2)}) async-start(), calls=%async_computation.47 | async-start | bytes 1966080 | tf_op jit(solution)/shard_map/reduce_scatter | solution.py:56
  1027.3 220.6 %all-reduce.8.cloned.1.call-start = ((), (), s32[]{:S(2)}) async-start(), calls=%async_computation.61 | async-start | bytes 7471104 | tf_op jit(solution)/shard_map/psum | solution.py:449
  (374 other events, 6623.4 us)
Sparse Core Ops, SparseCore 0:
  11.5 22.3 all-gather.13
  48.3 28.1 reduce-scatter.48
  103.9 20.8 reduce-scatter.72
  127.9 28.1 reduce-scatter.50
  159.0 20.7 reduce-scatter.74
  215.5 28.3 reduce-scatter.52
  271.3 20.8 reduce-scatter.76
  295.4 28.1 reduce-scatter.54
  326.5 20.7 reduce-scatter.78
  383.7 28.4 reduce-scatter.56
  451.9 28.1 reduce-scatter.58
  483.0 20.7 reduce-scatter.80
  551.8 28.1 reduce-scatter.60
  582.6 20.8 reduce-scatter.84
  645.7 28.1 reduce-scatter.62
  736.6 28.1 reduce-scatter.64
  767.3 20.8 reduce-scatter.88
  830.4 28.1 reduce-scatter.66
  895.5 20.7 reduce-scatter.90
  919.5 28.1 reduce-scatter.68
  950.2 20.8 reduce-scatter.92
  1012.7 34.3 all-reduce.5
  1072.4 28.1 reduce-scatter.70
  1104.8 142.9 all-reduce.7
  (14 shorter events, 279.4 us)
where the time goes:
time: 1270 us
  waiting for transfers between devices  660 us (52%)
  matrix products  211 us (17%)
  other arithmetic  128 us (10%)
  blocking collectives  124 us (10%)
  local copies, waits for them, and re-layouts  97 us (8%)
  starting transfers between devices  26 us (2%)
  between operations  19 us (1%)
    unnamed x50, waiting for transfers between devices  147 us
    reduce_scatter x6, waiting for transfers between devices, sum_rows(): lax.psum_scatter(text_part.astype(jnp.bfloat16), 'tensor', scatter_dimens...  139 us
    reduce_scatter x6, waiting for transfers between devices, sum_grads(): lax.psum_scatter(text_part.astype(jnp.bfloat16), 'tensor', scatter_dimens...  108 us
    psum x1, waiting for transfers between devices, per_device(): lax.psum(weight_totals[0].astype(jnp.bfloat16), 'dp').astype(jnp.float32)  96 us
    unnamed x744, local copies, waits for them, and re-layouts  93.8 us
    all_gather x6, waiting for transfers between devices, gather_rows(): lax.all_gather(text_part, 'tensor', axis=1, tiled=True)  76.3 us
    ppermute x8, waiting for transfers between devices, from_behind(): return lax.ppermute(block, axis, route)  47.1 us
    psum x1, blocking collectives, per_device(): lax.psum((section_pick * norm_totals[0][None], section_pick * norm_totals...  46.6 us
  transfers between devices with their start and end apart: 50, of which 44 were waited for; matrix products, arithmetic and copies ran while one was open for 20% of the time, Pallas kernels for 0%

commit v1 on v0

v1 whole, which is shorter than its diff:
```python
import functools
import math

import jax
import jax.numpy as jnp
from jax import lax
from jax.experimental import pallas as pl
from jax.experimental.pallas import tpu as pltpu
from jax.sharding import PartitionSpec as P

HEAD_TEXT = 64
HEAD_LAYOUT = 16
EPSILON = 1e-05
NEGATIVE = -1e30
HIGH = lax.Precision.HIGHEST
MESH = pl.DeviceIdType.MESH
BF = jnp.bfloat16
F32 = jnp.float32
ANY = pl.BlockSpec(memory_space=pl.ANY)


def remote(src, dst, send, recv, device):
    return pltpu.make_async_remote_copy(
        src_ref=src, dst_ref=dst, send_sem=send, recv_sem=recv, device_id=device, device_id_type=MESH
    )


def greet(section, tensor, sections, tensors, extra=()):
    barrier = pltpu.get_barrier_semaphore()
    for g in range(sections):
        for q in range(tensors):

            @pl.when((section != g) | (tensor != q))
            def _():
                pl.semaphore_signal(
                    barrier, inc=1, device_id={"section": g, "tensor": q}, device_id_type=MESH
                )

    for device in extra:
        pl.semaphore_signal(barrier, inc=1, device_id=device, device_id_type=MESH)
    pl.semaphore_wait(barrier, sections * tensors - 1 + len(extra))


def fetch_kernel(sections, tensors, dp, shared, *refs):
    n_weights = len(shared)
    sources = (refs[0:2], refs[2:4])
    weights = refs[4 : 4 + n_weights]
    pages = refs[4 + n_weights : 6 + n_weights]
    full = refs[6 + n_weights : 6 + 2 * n_weights]
    page_send, page_recv, w_send, w_recv, own_sem = refs[6 + 2 * n_weights :]
    section, d, t = lax.axis_index("section"), lax.axis_index("dp"), lax.axis_index("tensor")
    sibling = t + 1 - 2 * (t % 2)
    partner = (t + tensors // 2) % tensors
    mate = d + 1 - 2 * (d % 2)
    half = d % 2
    length = sources[0][0].shape[1]
    greet(section, t, sections, tensors, ({"dp": mate},))

    def rows(ref, i, which):
        count = ref.shape[1] // 2
        if not shared[i]:
            return ref
        return ref.at[:, pl.ds(pl.multiple_of(which * count, 16), count)]

    def part(ref, i, slot, which):
        if not shared[i]:
            return ref.at[slot]
        count = ref.shape[1] // 2
        return ref.at[slot, pl.ds(pl.multiple_of(which * count, 16), count)]

    def own_part(i):
        if not shared[i]:
            return weights[i]
        count = weights[i].shape[0] // 2
        return weights[i].at[pl.ds(pl.multiple_of(half * count, 16), count)]

    def token_slot(a, index):
        start = pl.multiple_of(index * length, length)
        return pages[a].at[pl.ds(start, length)] if a == 0 else pages[a].at[:, pl.ds(start, length)]

    def over_pages(act):
        for g in range(sections):
            for j in range(2):
                target = 2 * j + section
                here = (section == g) & (t == target)
                for a in range(2):
                    act(g, j, a, target, here)

    def page_start(g, j, a, target, here):
        src, dst = sources[g][a].at[j], token_slot(a, t)

        @pl.when(here)
        def _():
            pltpu.make_async_copy(src, dst, page_recv.at[a, t]).start()

        @pl.when(jnp.logical_not(here))
        def _():
            remote(
                src, dst, page_send.at[g, j, a], page_recv.at[a, t], {"section": g, "tensor": target}
            ).start()

    def page_sent(g, j, a, target, here):
        @pl.when(jnp.logical_not(here))
        def _():
            remote(
                sources[g][a].at[j], token_slot(a, t), page_send.at[g, j, a], page_recv.at[a, t],
                {"section": g, "tensor": target},
            ).wait_send()

    over_pages(page_start)

    def to_partner(i):
        return remote(
            own_part(i), part(full[i], i, t, half), w_send.at[0, i], w_recv.at[0, i], {"tensor": partner}
        )

    def to_sibling(i):
        return remote(
            weights[i], full[i].at[t], w_send.at[1, i], w_recv.at[1, i], {"tensor": sibling}
        )

    def to_mate(i):
        ref = part(full[i], i, partner, half)
        return remote(ref, ref, w_send.at[2, i], w_recv.at[2, i], {"dp": mate})

    def on_first(i):
        ref = part(full[i], i, partner, half)
        return remote(ref, ref, w_send.at[3, i], w_recv.at[3, i], {"tensor": sibling})

    def on_second(i):
        ref = part(full[i], i, partner, 1 - half)
        return remote(ref, ref, w_send.at[4, i], w_recv.at[4, i], {"tensor": sibling})

    def keep(i):
        return pltpu.make_async_copy(weights[i], full[i].at[t], own_sem.at[i])

    for i in range(n_weights):
        to_partner(i).start()
        to_sibling(i).start()
        keep(i).start()
    for i in range(n_weights):
        to_partner(i).wait_recv()
        on_first(i).start()
        if shared[i]:
            to_mate(i).start()
    for i in range(n_weights):
        if shared[i]:
            to_mate(i).wait_recv()
            on_second(i).start()
    for i in range(n_weights):
        keep(i).wait()
        to_sibling(i).wait()
        to_partner(i).wait_send()
        on_first(i).wait()
        if shared[i]:
            to_mate(i).wait_send()
            on_second(i).wait()
    over_pages(page_sent)
    for a in range(2):
        for q in range(tensors):
            slot = token_slot(a, q)
            remote(slot, slot, page_send.at[0, 0, a], page_recv.at[a, q], {"tensor": sibling}).wait_recv()


def fetch(mesh, text_in, layout_in, text_cot, layout_cot, weights):
    sections, dp, tensors = mesh.shape["section"], mesh.shape["dp"], mesh.shape["tensor"]
    length = text_in.shape[1] * tensors
    shared = tuple(dp % 2 == 0 and w.shape[0] >= 512 for w in weights)
    n = len(weights)
    shapes = (
        jax.ShapeDtypeStruct((length, text_in.shape[2]), BF),
        jax.ShapeDtypeStruct((layout_in.shape[1], length), BF),
    ) + tuple(jax.ShapeDtypeStruct((tensors,) + w.shape, BF) for w in weights)
    outs = pl.pallas_call(
        functools.partial(fetch_kernel, sections, tensors, dp, shared),
        out_shape=shapes,
        in_specs=[ANY] * (4 + n),
        out_specs=[ANY] * len(shapes),
        scratch_shapes=[
            pltpu.SemaphoreType.DMA((sections, 2, 2)),
            pltpu.SemaphoreType.DMA((2, tensors)),
            pltpu.SemaphoreType.DMA((5, n)),
            pltpu.SemaphoreType.DMA((5, n)),
            pltpu.SemaphoreType.DMA((n,)),
        ],
        compiler_params=pltpu.CompilerParams(collective_id=0, has_side_effects=True),
        name="fetch",
    )(text_in, layout_in, text_cot, layout_cot, *weights)
    return outs[0], outs[1], outs[2:]


def return_kernel(sections, tensors, text, layout, text_out, layout_out, grad_out, layout_grad_out, send, recv):
    section, t = lax.axis_index("section"), lax.axis_index("tensor")
    length = text_out.shape[1]
    greet(section, t, sections, tensors)
    micro, page = t % 2, t // 2
    kinds = ((grad_out, layout_grad_out), (text_out, layout_out))

    def source(a, q):
        start = q * length
        return text.at[pl.ds(start, length)] if a == 0 else layout.at[:, pl.ds(start, length)]

    def each(act):
        for g in range(sections):
            for q in range(tensors):
                for a in range(2):
                    @pl.when(section == g)
                    def _():
                        act(g, q, a, (micro == g) & (t == q))

    def start(g, q, a, here):
        src, dst = source(a, q), kinds[g][a].at[page]

        @pl.when(here)
        def _():
            pltpu.make_async_copy(src, dst, recv.at[g, a, page]).start()

        @pl.when(jnp.logical_not(here))
        def _():
            remote(src, dst, send.at[q, a], recv.at[g, a, page], {"section": micro, "tensor": q}).start()

    def sent(g, q, a, here):
        @pl.when(jnp.logical_not(here))
        def _():
            remote(
                source(a, q), kinds[g][a].at[page], send.at[q, a], recv.at[g, a, page],
                {"section": micro, "tensor": q},
            ).wait_send()

    each(start)
    each(sent)
    for g in range(sections):
        for a in range(2):
            for j in range(2):
                dst = kinds[g][a].at[j]
                remote(dst, dst, send.at[0, a], recv.at[g, a, j], {"tensor": (t + 1) % tensors}).wait_recv()


def give_back(mesh, text, layout):
    sections, tensors = mesh.shape["section"], mesh.shape["tensor"]
    length = text.shape[0] // tensors
    text_shape = jax.ShapeDtypeStruct((2, length, text.shape[1]), BF)
    layout_shape = jax.ShapeDtypeStruct((2, layout.shape[0], length), BF)
    return pl.pallas_call(
        functools.partial(return_kernel, sections, tensors),
        out_shape=(text_shape, layout_shape, text_shape, layout_shape),
        in_specs=[ANY] * 2,
        out_specs=[ANY] * 4,
        scratch_shapes=[
            pltpu.SemaphoreType.DMA((tensors, 2)),
            pltpu.SemaphoreType.DMA((sections, 2, 2)),
        ],
        compiler_params=pltpu.CompilerParams(collective_id=1, has_side_effects=True),
        name="give_back",
    )(text, layout)


def norm_forward(summed, gain, offset):
    center = summed - jnp.mean(summed, axis=-1, keepdims=True)
    inverse = lax.rsqrt(jnp.mean(center * center, axis=-1, keepdims=True) + EPSILON)
    normed = center * inverse
    return (normed * gain + offset, normed, inverse)


def norm_backward(upstream, normed, inverse, gain):
    scaled = upstream * gain
    mean_scaled = jnp.mean(scaled, axis=-1, keepdims=True)
    mean_product = jnp.mean(scaled * normed, axis=-1, keepdims=True)
    downstream = inverse * (scaled - mean_scaled - normed * mean_product)
    return (downstream, jnp.sum(upstream * normed, axis=0), jnp.sum(upstream, axis=0))


def activation(values):
    return jax.nn.gelu(values, approximate=False)


def mm(spec, a, b):
    return jnp.einsum(spec, a, b, preferred_element_type=F32)


def layer_forward(rows, weights, norms, valid):
    heads = []
    for b in range(2):
        qkv = mm("ld,tnd->ltn", rows[b], weights[b][0]).astype(BF)
        heads.append(qkv.reshape(qkv.shape[0], qkv.shape[1], 3, -1, (HEAD_TEXT, HEAD_LAYOUT)[b]))
    scores = mm("qthd,kthd->thqk", heads[0][:, :, 0], heads[0][:, :, 1]) * (1.0 / math.sqrt(HEAD_TEXT))
    scores = scores + mm("qthd,kthd->thqk", heads[1][:, :, 0], heads[1][:, :, 1]) * (
        1.0 / math.sqrt(HEAD_LAYOUT)
    )
    scores = jnp.where(valid[None, None, None, :], scores, NEGATIVE)
    highest = jnp.max(scores, axis=-1, keepdims=True)
    raised = jnp.exp(scores - highest)
    probs = (raised / jnp.sum(raised, axis=-1, keepdims=True)).astype(BF)
    outs, kept = [], []
    for b in range(2):
        gains, biases = norms[b]
        context = mm("thqk,kthd->qthd", probs, heads[b][:, :, 2]).astype(BF)
        context = context.reshape(context.shape[0], context.shape[1], -1)
        attended = mm("ltn,tnd->ld", context, weights[b][1])
        hidden, n1, r1 = norm_forward(rows[b].astype(F32) + attended, gains[0], biases[0])
        low = hidden.astype(BF)
        pre = mm("ld,tdn->ltn", low, weights[b][2])
        active = activation(pre).astype(BF)
        fed = mm("ltn,tnd->ld", active, weights[b][3])
        out, n2, r2 = norm_forward(hidden + fed, gains[1], biases[1])
        outs.append(out.astype(BF))
        kept.append((context, n1, r1, low, pre, active, n2, r2))
    return tuple(outs), (tuple(heads), probs, tuple(kept))


def layer_backward(saved, grads, weights, norms):
    heads, probs, kept = saved
    probs_f = probs.astype(F32)
    norm_grads, operands, dz_ones, score_grads, context_grads = [], [], [], [], []
    for b in range(2):
        gains, biases = norms[b]
        context, n1, r1, low, pre, active, n2, r2 = kept[b]
        dz_two, g2, b2 = norm_backward(grads[b].astype(F32), n2, r2, gains[1])
        gf = dz_two.astype(BF)
        d_active = mm("ld,tnd->ltn", gf, weights[b][3])
        d_pre = jax.vjp(activation, pre)[1](d_active)[0].astype(BF)
        d_hidden = dz_two + mm("ltn,tdn->ld", d_pre, weights[b][2])
        dz_one, g1, b1 = norm_backward(d_hidden, n1, r1, gains[0])
        ga = dz_one.astype(BF)
        d_context = mm("ld,tnd->ltn", ga, weights[b][1]).astype(BF)
        d_context = d_context.reshape(heads[b][:, :, 2].shape)
        d_probs = mm("qthd,kthd->thqk", d_context, heads[b][:, :, 2])
        inner = jnp.sum(probs_f * d_probs, axis=-1, keepdims=True)
        score_grads.append((probs_f * (d_probs - inner)).astype(BF))
        context_grads.append(d_context)
        dz_ones.append(dz_one)
        norm_grads.append((jnp.stack([g1, g2]), jnp.stack([b1, b2])))
        operands.append([gf, d_pre, ga])
    total = (score_grads[0].astype(F32) + score_grads[1].astype(F32)).astype(BF)
    reaching = (total, score_grads[1])
    downs, out_operands = [], []
    for b in range(2):
        scale = 1.0 / math.sqrt((HEAD_TEXT, HEAD_LAYOUT)[b])
        dq = (mm("thqk,kthd->qthd", reaching[b], heads[b][:, :, 1]) * scale).astype(BF)
        dk = (mm("thqk,qthd->kthd", reaching[b], heads[b][:, :, 0]) * scale).astype(BF)
        dv = mm("thqk,qthd->kthd", probs, context_grads[b]).astype(BF)
        stacked = jnp.stack([dq, dk, dv], axis=2)
        stacked = stacked.reshape(stacked.shape[0], stacked.shape[1], -1)
        down = dz_ones[b] + mm("ltn,tnd->ld", stacked, weights[b][0])
        downs.append(down.astype(BF))
        out_operands.append((stacked, *operands[b]))
    return tuple(downs), tuple(out_operands), tuple(norm_grads)


def zeros_like_tree(shapes):
    return jax.tree.map(lambda s: jnp.zeros(s.shape, s.dtype), shapes)


def reduce_shard(grad, t, tensors):
    sibling = [(i, i + 1 - 2 * (i % 2)) for i in range(tensors)]
    partner = [(i, (i + tensors // 2) % tensors) for i in range(tensors)]
    pairs = grad.reshape((2, tensors // 2) + grad.shape[1:])
    core, chip = t % 2, t // 2
    theirs = lax.dynamic_index_in_dim(pairs, 1 - core, 1, keepdims=False)
    mine = lax.dynamic_index_in_dim(pairs, core, 1, keepdims=False)
    summed = (mine.astype(F32) + lax.ppermute(theirs, "tensor", sibling).astype(F32)).astype(BF)
    theirs = lax.dynamic_index_in_dim(summed, 1 - chip, 0, keepdims=False)
    mine = lax.dynamic_index_in_dim(summed, chip, 0, keepdims=False)
    summed = (mine.astype(F32) + lax.ppermute(theirs, "tensor", partner).astype(F32)).astype(BF)
    return lax.psum(summed, "dp").astype(F32)


def per_device(
    mesh,
    text_input,
    layout_input,
    text_cotangent,
    layout_cotangent,
    page_counts,
    pad_mask,
    lang_ids,
    lang_table,
    text_project,
    text_outward,
    text_upward,
    text_downward,
    text_gains,
    text_biases,
    layout_project,
    layout_outward,
    layout_upward,
    layout_downward,
    layout_gains,
    layout_biases,
):
    section, t = lax.axis_index("section"), lax.axis_index("tensor")
    tensors = mesh.shape["tensor"]
    micro, page = t % 2, t // 2

    def flat(project):
        return jnp.transpose(project[0], (1, 2, 0)).reshape(-1, project.shape[1])

    own_ids = lax.dynamic_index_in_dim(lang_ids, section, 0, keepdims=False)
    groups = jnp.arange(lang_table.shape[0], dtype=jnp.int32)
    onehot = (own_ids[:, None] == groups[None, :]).astype(F32)
    lang_rows = jnp.dot(onehot, lang_table, precision=HIGH)
    embedded = (text_input[0].astype(F32) + lang_rows[:, None, :]).astype(BF)
    flipped = lambda block: jnp.transpose(block[0], (0, 2, 1))
    shards = (
        flat(text_project), text_outward[0], text_upward[0], text_downward[0],
        flat(layout_project), layout_outward[0], layout_upward[0], layout_downward[0],
    )
    text_page, layout_page, full = fetch(
        mesh, embedded, flipped(layout_input), text_cotangent[0], flipped(layout_cotangent), shards
    )
    weights = (full[0:4], full[4:8])
    norms = ((text_gains[0], text_biases[0]), (layout_gains[0], layout_biases[0]))
    counts = page_counts[micro, page]
    positions = jnp.arange(pad_mask.shape[2], dtype=jnp.int32)
    valid = (positions < counts) & ((pad_mask[micro, page] == 1) | (positions == 0))
    arrived = (text_page, layout_page.T)

    def run(rows):
        return (rows,) + layer_forward(rows, weights, norms, valid)

    shapes = jax.eval_shape(run, arrived)
    kept = lax.cond(section == 0, run, lambda rows: zeros_like_tree(shapes), arrived)
    hopped = tuple(lax.ppermute(block, "section", [(0, 1)]) for block in kept[1])
    rows, outs, saved = lax.cond(section == 1, lambda old, got: run(got), lambda old, got: old, kept, hopped)

    def back(grads):
        return layer_backward(saved, grads, weights, norms)

    back_shapes = jax.eval_shape(back, arrived)
    first = lax.cond(section == 1, back, lambda grads: zeros_like_tree(back_shapes), arrived)
    hopped = tuple(lax.ppermute(block, "section", [(1, 0)]) for block in first[0])
    downs, operands, norm_grads = lax.cond(
        section == 0, lambda old, got: back(got), lambda old, got: old, first, hopped
    )
    _, _, kept = saved
    grads = []
    for b in range(2):
        stacked, gf, d_pre, ga = operands[b]
        context, n1, r1, low, pre, active, n2, r2 = kept[b]
        grads.append((
            mm("ltn,ld->tnd", stacked, rows[b]).astype(BF),
            mm("ltn,ld->tnd", context, ga).astype(BF),
            mm("ld,ltn->tdn", low, d_pre).astype(BF),
            mm("ltn,ld->tnd", active, gf).astype(BF),
        ))
    final = tuple(jnp.where(section == 0, d, o) for d, o in zip(downs, outs))
    text_out, layout_out, text_grad, layout_grad = give_back(mesh, final[0], final[1].T)
    summed = [[reduce_shard(g, t, tensors) for g in per_stream] for per_stream in grads]

    own_group = lax.dynamic_index_in_dim(lang_ids[:, page], micro, 0, keepdims=False)
    page_sum = jnp.where(section == 0, jnp.sum(downs[0].astype(F32), axis=0), 0.0)
    lang_grad = (groups == own_group).astype(F32)[:, None] * page_sum[None, :]
    pick = (jnp.arange(2, dtype=jnp.int32) == section).astype(F32)[:, None, None]
    small = lax.psum(
        tuple(pick * member[None] for pair in norm_grads for member in pair) + (lang_grad,),
        ("section", "dp", "tensor"),
    )

    def own_row(stacked):
        return lax.dynamic_slice_in_dim(stacked, section, 1, 0)

    def unflat(grad, like):
        return jnp.transpose(grad.reshape(like.shape[2], like.shape[3], like.shape[1]), (2, 0, 1))[None]

    unflip = lambda block: jnp.transpose(block, (0, 2, 1))[None]
    return (
        text_out[None], unflip(layout_out), text_grad[None], unflip(layout_grad), small[4],
        unflat(summed[0][0], text_project), summed[0][1][None], summed[0][2][None], summed[0][3][None],
        own_row(small[0]), own_row(small[1]),
        unflat(summed[1][0], layout_project), summed[1][1][None], summed[1][2][None], summed[1][3][None],
        own_row(small[2]), own_row(small[3]),
    )


def solution(mesh):
    tokens = P("section", "dp", "tensor", None)
    weight_specs = (
        P("section", None, None, "tensor"), P("section", "tensor", None), P("section", None, "tensor"),
        P("section", "tensor", None), P("section", None, None), P("section", None, None),
    )
    in_specs = (tokens,) * 4 + (P(None, "dp"), P(None, "dp", None), P(None, "dp"), P()) + weight_specs * 2
    out_specs = (tokens,) * 4 + (P(),) + weight_specs * 2
    return jax.shard_map(
        functools.partial(per_device, mesh), mesh=mesh, in_specs=in_specs, out_specs=out_specs, check_vma=False
    )
```

time: 1270 us -> 862 us (0.68)
  waiting for transfers between devices: 660 us -> 351 us
  Pallas kernels: 0 us -> 129 us
  blocking collectives: 124 us -> 47.3 us
  other arithmetic: 128 us -> 72 us
  local copies, waits for them, and re-layouts: 97 us -> 42.5 us
  matrix products: 211 us -> 170 us
    reduce_scatter x12 -> x0, waiting for transfers between devices: 248 us -> none  [the longest x6 139 us: sum_rows(): lax.psum_scatter(text_part.astype(jnp.bfloat16), 'tensor', scatter_dimens...]
    ppermute x12 -> x20, waiting for transfers between devices: 47.1 us -> 279 us  [the longest x2 195 us: per_device(): lax.ppermute(block, 'section', [(1, 0)])]
    unnamed x50 -> x2, waiting for transfers between devices: 147 us -> 0.03 us
    pallas_call x0 -> x2, Pallas kernels: none -> 129 us  [the longest x1 116 us: fetch(): pl.pallas_call(functools.partial(fetch_kernel, sections, tensors, dp, sha...]
    all_gather x12 -> x0, waiting for transfers between devices: 123 us -> none  [the longest x6 76.3 us: gather_rows(): lax.all_gather(text_part, 'tensor', axis=1, tiled=True)]
    unnamed x744 -> x70, local copies, waits for them, and re-layouts: 93.8 us -> 9.08 us
    all_gather x12 -> x0, blocking collectives: 77.7 us -> none  [the longest x6 40.3 us: gather_rows(): lax.all_gather(layout_part, 'tensor', axis=1, tiled=True)]
    dot_general x116 -> x34, matrix products: 211 us -> 157 us  [the longest x33 157 us: mm(): return jnp.einsum(spec, a, b, preferred_element_type=F32)]
  transfers between devices with their start and end apart: 50 -> 22, of which waited for: 44 -> 7; matrix products, arithmetic and copies ran while one was open for 20% -> 8% of each run, Pallas kernels for 0% -> 1%
where the time goes in v1:
time: 862 us; the launch traced here: 855 us
  waiting for transfers between devices  351 us (41%)
  matrix products  170 us (20%)
  Pallas kernels  129 us (15%)
  other arithmetic  72 us (8%)
  blocking collectives  47.3 us (5%)
  local copies, waits for them, and re-layouts  42.5 us (5%)
  starting transfers between devices  15.8 us (2%)
  between operations  15.2 us (2%)
  loops' own time  12.7 us (1%)
    ppermute x2, waiting for transfers between devices, per_device(): lax.ppermute(block, 'section', [(1, 0)])  195 us
    dot_general x33, matrix products, mm(): return jnp.einsum(spec, a, b, preferred_element_type=F32)  157 us
    pallas_call x1, Pallas kernels, fetch(): pl.pallas_call(functools.partial(fetch_kernel, sections, tensors, dp, sha...  116 us
    psum x2, waiting for transfers between devices, reduce_shard(): return lax.psum(summed, 'dp').astype(F32)  71.7 us
    ppermute x8, waiting for transfers between devices, reduce_shard(): lax.ppermute(theirs, 'tensor', partner).astype(F32)  63.7 us
    psum x1, blocking collectives, per_device(): lax.psum(tuple((pick * member[None] for pair in norm_grads for member in...  47.3 us
    ppermute x2, waiting for transfers between devices, per_device(): lax.ppermute(block, 'section', [(0, 1)])  20.5 us
  transfers between devices with their start and end apart: 22, of which 7 were waited for; matrix products, arithmetic and copies ran while one was open for 8% of the time, Pallas kernels for 1%

profile of v1, /device:TPU:0, one launch (start us, length us, event | category | flops | bytes accessed | tf_op | source)
XLA Modules:
  0.0 855.1 jit_solution(3316247286933710913)
XLA Ops:
  12.6 116.2 %fetch.1 = (bf16[512,768]{1,0:T(8,128)(2,1)S(1)}, bf16[192,512]{1,0:T(8,128)(2,1)S(1)}, bf16[4,576,768]{2,1,0:T(8,128)(2,1)}, bf16[4,192,768]{2,1,0:T(8,128)(2,1...) custom-call(bf16[2,128,768]{2,1,0:T(8,128)(2,1)} %fusion.243.refs_0_, ...), custom_call_target="tpu_custom_call" | custom-call | tf_op jit(solution)/shard_map/fetch/pallas_call | solution.py:174
  130.0 85.1 %conditional.4 = (bf16[512,768]{1,0:T(8,128)(2,1)}, bf16[512,192]{0,1:T(8,128)(2,1)S(1)}, bf16[512,768]{1,0:T(8,128)(2,1)}, bf16[512,192]{0,1:T(8,128)(2,1)}, bf...) conditional(s32[]{:T(128)} %convert_element_type.541, () %tuple.47, ...), branch_computations={%region_0.1_spmd, %region_1.12_spmd} | conditional | flops 8873610240 | bytes 192583328 | solution.py:422
  130.0 5.7 convolution_convert_fusion
  135.7 7.7 fusion.24
  143.7 11.1 %fusion.276 = (f32[4,3,512]{2,1,0:T(4,128)S(1)}, f32[4,3,512,512]{2,3,1,0:T(8,128)}) fusion(f32[4,3,512,512]{2,3,1,0:T(8,128)} %fusion.24, pred[512]{0:T(512)(128)(4,1)S(1)} %get-tuple-element.295, bf16[512,4,3,3,16]{0,4,3,2,1:T(8,128)(2,1)S(1)} %bitcast.624), kind=kOutput, calls=%fused_computation.565 | convolution fusion | flops 119538176 | bytes 25584128 | tf_op jit(solution)/shard_map/cond/branch_1_fun/sub | solution.py:292
  154.8 9.2 %divide_convert_fusion = bf16[4,3,512,512]{2,3,1,0:T(8,128)(2,1)} fusion(f32[4,3,512,512]{2,3,1,0:T(8,128)} %get-tuple-element.786, f32[4,3,512]{2,1,0:T(4,128)S(1)} %get-tuple-element.785), kind=kLoop, calls=%fused_computation.1 | loop fusion | flops 6291456 | bytes 18898944 | tf_op jit(solution)/shard_map/cond/branch_1_fun/convert_element_type | solution.py:293
  177.2 5.2 convolution_convert_fusion.1
  186.2 20.1 %fusion.3 = (bf16[512,4,768]{2,0,1:T(8,128)(2,1)}, f32[512,4,768]{2,0,1:T(8,128)}) fusion(bf16[4,768,768]{2,1,0:T(8,128)(2,1)S(1)} %bitcast.743, bf16[512,768]{1,0:T(8,128)(2,1)} %get-tuple-element.866), kind=kOutput, calls=%fused_computation.7 | convolution fusion | flops 2518155264 | bytes 14942208 | tf_op jit(solution)/shard_map/cond/branch_1_fun/ld,tdn->ltn/dot_general | solution.py:278
  217.7 20.5 %collective-permute-done.1 = bf16[512,192]{0,1:T(8,128)(2,1)S(1)} collective-permute-done((bf16[512,192]{0,1:T(8,128)(2,1)}, bf16[512,192]{0,1:T(8,128)(2,1)S(1)}, u32[]{:S(2)}, u32[]{:S(2)}) %collective-permute-start.1) | collective-permute-done | bytes 196640 | tf_op jit(solution)/shard_map/ppermute | solution.py:423
  238.3 6.1 conditional.5
  244.3 15.7 %conditional.6 = (bf16[512,768]{1,0:T(8,128)(2,1)}, bf16[512,192]{0,1:T(8,128)(2,1)}, bf16[512,4,576]{0,2,1:T(8,128)(2,1)}, bf16[512,768]{1,0:T(8,128)(2,1)}, bf...) conditional(s32[]{:T(128)} %convert_element_type.542, () %tuple.46, ...), branch_computations={%region_24.25_spmd, %region_25.44_spmd} | conditional | flops 11175008256 | bytes 304827648 | solution.py:430
  262.7 194.8 %collective-permute-done.3 = bf16[512,192]{0,1:T(8,128)(2,1)S(1)} collective-permute-done((bf16[512,192]{0,1:T(8,128)(2,1)}, bf16[512,192]{0,1:T(8,128)(2,1)S(1)}, u32[]{:S(2)}, u32[]{:S(2)}) %collective-permute-start.3) | collective-permute-done | bytes 196640 | tf_op jit(solution)/shard_map/ppermute | solution.py:431
  457.5 105.1 %conditional.7 = ((bf16[512,768]{1,0:T(8,128)(2,1)}, bf16[512,192]{0,1:T(8,128)(2,1)}, bf16[512,4,576]{0,2,1:T(8,128)(2,1)}, bf16[512,768]{1,0:T(8,128)(2,1)}, b...) conditional(s32[]{:T(128)} %convert_element_type.541, ...), branch_computations={%region_44.45_spmd, %region_45.64_spmd} | conditional | flops 11175008256 | bytes 305122560 | solution.py:432
  460.9 6.3 fusion.187
  475.7 5.5 fusion.150
  495.3 19.8 %fusion.156 = bf16[512,4,768]{2,0,1:T(8,128)(2,1)} fusion(f32[512,4,768]{2,0,1:T(8,128)} %get-tuple-element.352, bf16[4,768,768]{2,1,0:T(8,128)(2,1)S(1)} %bitcast.757, bf16[512,768]{1,0:T(8,128)(2,1)S(1)} %fusion.232), kind=kOutput, calls=%fused_computation.334 | convolution fusion | flops 2529165312 | bytes 14942208 | tf_op jit(solution)/shard_map/cond/branch_1_fun/ld,tnd->ltn/dot_general | solution.py:278
  523.4 12.2 %fusion.201 = bf16[512,4,1,3,64]{0,4,3,1,2:T(8,128)(2,1)S(1)} fusion(bf16[4,3,512,512]{2,3,1,0:T(8,128)(2,1)} %copy-done.2, bf16[4,3,512,512]{2,3,1,0:T(8,128)(2,1)} %get-tuple-element.356, bf16[512,4,3,64]{0,3,2,1:T(8,128)(2,1)S(1)} %bitcast.650, bf16[512,4,3,3,64]{0,4,3,2,1:T(8,128)(2,1)} %get-tuple-element.660), kind=kOutput, calls=%fused_computation.397 | convolution fusion | flops 1240209920 | bytes 23592960 | tf_op jit(solution)/shard_map/cond/branch_1_fun/thqk,kthd->qthd/dot_general | solution.py:278
  535.6 13.7 %fusion.204 = bf16[512,4,1,3,64]{0,4,3,1,2:T(8,128)(2,1)} fusion(bf16[4,3,512,512]{2,3,1,0:T(8,128)(2,1)} %copy-done.2, bf16[4,3,512,512]{2,3,1,0:T(8,128)(2,1)} %get-tuple-element.356, bf16[512,4,3,64]{0,3,2,1:T(8,128)(2,1)S(1)} %bitcast.651, bf16[512,4,3,3,64]{0,4,3,2,1:T(8,128)(2,1)} %get-tuple-element.660), kind=kOutput, calls=%fused_computation.398 | convolution fusion | flops 1240209920 | bytes 23592960 | tf_op jit(solution)/shard_map/cond/branch_1_fun/thqk,qthd->kthd/dot_general | solution.py:278
  628.6 14.5 %collective-permute-done.5 = bf16[576,768]{1,0:T(8,128)(2,1)S(1)} collective-permute-done((bf16[576,768]{1,0:T(8,128)(2,1)S(1)}, bf16[576,768]{1,0:T(8,128)(2,1)S(1)}, u32[]{:S(2)}, u32[]{:S(2)}) %collective-permute-start.5) | collective-permute-done | bytes 884768 | tf_op jit(solution)/shard_map/ppermute | solution.py:364
  644.1 24.1 %collective-permute-done.11 = bf16[768,768]{1,0:T(8,128)(2,1)S(1)} collective-permute-done((bf16[768,768]{1,0:T(8,128)(2,1)S(1)}, bf16[768,768]{1,0:T(8,128)(2,1)S(1)}, u32[]{:S(2)}, u32[]{:S(2)}) %collective-permute-start.11) | collective-permute-done | bytes 1179680 | tf_op jit(solution)/shard_map/ppermute | solution.py:364
  669.6 23.0 %collective-permute-done.9 = bf16[768,768]{1,0:T(8,128)(2,1)S(1)} collective-permute-done((bf16[768,768]{1,0:T(8,128)(2,1)S(1)}, bf16[768,768]{1,0:T(8,128)(2,1)S(1)}, u32[]{:S(2)}, u32[]{:S(2)}) %collective-permute-start.9) | collective-permute-done | bytes 1179680 | tf_op jit(solution)/shard_map/ppermute | solution.py:364
  699.7 12.6 %give_back.1 = (bf16[2,128,768]{2,1,0:T(8,128)(2,1)}, bf16[2,192,128]{2,1,0:T(8,128)(2,1)}, bf16[2,128,768]{2,1,0:T(8,128)(2,1)}, bf16[2,192,128]{2,1,0:T(8,128)(2,1)}) custom-call(bf16[512,768]{1,0:T(8,128)(2,1)} %broadcast_select_fusion.text, bf16[192,512]{1,0:T(8,128)(2,1)} %select_bitcast_fusion.layout), custom_call_target="tpu_custom_call" | custom-call | tf_op jit(solution)/shard_map/give_back/pallas_call | solution.py:244
  713.8 47.3 %all-reduce = (f32[8,768]{1,0:T(8,128)}, f32[2,2,768]{2,1,0:T(2,128)S(1)}, f32[2,2,768]{2,1,0:T(2,128)S(1)}, f32[2,2,192]{2,1,0:T(2,128)S(1)}, f32[2,2,192]{2,1,0:T(2,128)S(1)}) all-reduce(f32[8,768]{1,0:T(8,128)S(1)} %broadcast_multiply_fusion.24, ...), channel_id=1, replica_groups=mesh['section'=2,'dp'=4,'tensor'=4] {'section','dp','tensor'}, use_global_device_ids=true, to_apply=%region_65.66 | all-reduce | flops 13824 | bytes 110592 | tf_op jit(solution)/shard_map/psum | solution.py:454
  765.2 71.7 %all-reduce.8.cloned.1.call-done = (bf16[1,768,3,192]{1,3,2,0:T(8,128)(2,1)}, bf16[1,192,768]{2,1,0:T(8,128)(2,1)}, bf16[1,768,768]{2,1,0:T(8,128)(2,1)}, bf16[1...) async-done(((bf16[1,768,3,192]{1,3,2,0:T(8,128)(2,1)}, bf16[1,192,768]{2,1,0:T(8,128)(2,1)}, bf16[1,768,768]{2,1,0:T(8,128)(2,1)}, ...) | async-done | bytes 3686416 | tf_op jit(solution)/shard_map/psum | solution.py:365
  (340 shorter events, 185.9 us)
Async XLA Ops:
  7.2 755.1 %all-reduce.6.cloned.1.call-start = ((), (), s32[]{:S(2)}) async-start(), calls=%async_computation | async-start | bytes 196608 | tf_op jit(solution)/shard_map/psum | solution.py:365
  12.6 116.3 %copy-start.86 = (f32[1,2,768]{2,1,0:T(2,128)S(1)}, f32[1,2,768]{2,1,0:T(2,128)}, u32[]{:S(2)}) copy-start(f32[1,2,768]{2,1,0:T(2,128)} %param.41) | copy-start | bytes 18436
  12.6 116.3 %copy-start.91 = (f32[1,2,192]{2,1,0:T(2,128)S(1)}, f32[1,2,192]{2,1,0:T(2,128)}, u32[]{:S(2)}) copy-start(f32[1,2,192]{2,1,0:T(2,128)} %param.47) | copy-start | bytes 4612
  215.0 23.2 %collective-permute-start = (bf16[512,768]{1,0:T(8,128)(2,1)}, bf16[512,768]{1,0:T(8,128)(2,1)S(1)}, u32[]{:S(2)}, u32[]{:S(2)}) collective-permute-start(bf16[512,768]{1,0:T(8,128)(2,1)} %get-tuple-element.454), channel_id=1, source_target_pairs={{0,16},{1,17},{2,18},{3,19},{4,20},{5,21},{6,22},{7,23},{8,24},{9,... | collective-permute-start | bytes 2359304 | tf_op jit(solution)/shard_map/ppermute | solution.py:423
  216.4 21.9 %collective-permute-start.1 = (bf16[512,192]{0,1:T(8,128)(2,1)}, bf16[512,192]{0,1:T(8,128)(2,1)S(1)}, u32[]{:S(2)}, u32[]{:S(2)}) collective-permute-start(bf16[512,192]{0,1:T(8,128)(2,1)} %get-tuple-element.455), channel_id=1, source_target_pairs={{0,16},{1,17},{2,18},{3,19},{4,20},{5,21},{6,22},{7,23},{8,24},{9,... | collective-permute-start | bytes 589832 | tf_op jit(solution)/shard_map/ppermute | solution.py:423
  260.1 197.5 %collective-permute-start.2 = (bf16[512,768]{1,0:T(8,128)(2,1)}, bf16[512,768]{1,0:T(8,128)(2,1)S(1)}, u32[]{:S(2)}, u32[]{:S(2)}) collective-permute-start(bf16[512,768]{1,0:T(8,128)(2,1)} %get-tuple-element.469), channel_id=1, source_target_pairs={{16,0},{17,1},{18,2},{19,3},{20,4},{21,5},{22,6},{23,7},{24,8},{25... | collective-permute-start | bytes 2359304 | tf_op jit(solution)/shard_map/ppermute | solution.py:431
  261.4 196.2 %collective-permute-start.3 = (bf16[512,192]{0,1:T(8,128)(2,1)}, bf16[512,192]{0,1:T(8,128)(2,1)S(1)}, u32[]{:S(2)}, u32[]{:S(2)}) collective-permute-start(bf16[512,192]{0,1:T(8,128)(2,1)} %get-tuple-element.470), channel_id=1, source_target_pairs={{16,0},{17,1},{18,2},{19,3},{20,4},{21,5},{22,6},{23,7},{24,8},{25... | collective-permute-start | bytes 589832 | tf_op jit(solution)/shard_map/ppermute | solution.py:431
  564.0 29.9 %collective-permute-start.14 = (bf16[2,48,192]{2,1,0:T(8,128)(2,1)S(1)}, bf16[2,48,192]{2,1,0:T(8,128)(2,1)}, u32[]{:S(2)}, u32[]{:S(2)}) collective-permute-start(bf16[2,48,192]{2,1,0:T(8,128)(2,1)S(1)} %dynamic-slice_bitcast_fusion.12), channel_id=1, source_target_pairs={{0,1},{1,0},{2,3},{3,2},{4,5},{5,4},{6,7},{7,6},{8,9},{9,8},{10,11... | collective-permute-start | bytes 110600 | tf_op jit(solution)/shard_map/ppermute | solution.py:361
  566.7 35.5 %collective-permute-start.12 = (bf16[2,144,192]{2,1,0:T(8,128)(2,1)}, bf16[2,144,192]{2,1,0:T(8,128)(2,1)}, u32[]{:S(2)}, u32[]{:S(2)}) collective-permute-start(bf16[2,144,192]{2,1,0:T(8,128)(2,1)} %dynamic-slice_bitcast_fusion.8), channel_id=1, source_target_pairs={{0,1},{1,0},{2,3},{3,2},{4,5},{5,4},{6,7},{7,6},{8,9},{9,8},{10,11... | collective-permute-start | bytes 331784 | tf_op jit(solution)/shard_map/ppermute | solution.py:361
  569.0 34.8 %collective-permute-start.18 = (bf16[2,192,192]{2,1,0:T(8,128)(2,1)}, bf16[2,192,192]{2,1,0:T(8,128)(2,1)}, u32[]{:S(2)}, u32[]{:S(2)}) collective-permute-start(bf16[2,192,192]{2,1,0:T(8,128)(2,1)} %dynamic-slice_bitcast_fusion.7), channel_id=1, source_target_pairs={{0,1},{1,0},{2,3},{3,2},{4,5},{5,4},{6,7},{7,6},{8,9},{9,8},{10,11... | collective-permute-start | bytes 442376 | tf_op jit(solution)/shard_map/ppermute | solution.py:361
  571.9 32.9 %collective-permute-start.16 = (bf16[2,192,192]{2,1,0:T(8,128)(2,1)}, bf16[2,192,192]{2,1,0:T(8,128)(2,1)}, u32[]{:S(2)}, u32[]{:S(2)}) collective-permute-start(bf16[2,192,192]{2,1,0:T(8,128)(2,1)} %bitcast.226), channel_id=1, source_target_pairs={{0,1},{1,0},{2,3},{3,2},{4,5},{5,4},{6,7},{7,6},{8,9},{9,8},{10,11... | collective-permute-start | bytes 442376 | tf_op jit(solution)/shard_map/ppermute | solution.py:361
  579.3 38.9 %collective-permute-start.10 = (bf16[2,768,768]{2,1,0:T(8,128)(2,1)}, bf16[2,768,768]{2,1,0:T(8,128)(2,1)}, u32[]{:S(2)}, u32[]{:S(2)}) collective-permute-start(bf16[2,768,768]{2,1,0:T(8,128)(2,1)} %dynamic-slice_bitcast_fusion), channel_id=1, source_target_pairs={{0,1},{1,0},{2,3},{3,2},{4,5},{5,4},{6,7},{7,6},{8,9},{9,8},{10,11... | collective-permute-start | bytes 7077896 | tf_op jit(solution)/shard_map/ppermute | solution.py:361
  594.7 6.8 collective-permute-start.15
  601.6 12.5 %collective-permute-start.4 = (bf16[2,576,768]{2,1,0:T(8,128)(2,1)}, bf16[2,576,768]{2,1,0:T(8,128)(2,1)}, u32[]{:S(2)}, u32[]{:S(2)}) collective-permute-start(bf16[2,576,768]{2,1,0:T(8,128)(2,1)} %dynamic-slice_bitcast_fusion.1), channel_id=1, source_target_pairs={{0,1},{1,0},{2,3},{3,2},{4,5},{5,4},{6,7},{7,6},{8,9},{9,8},{10,11... | collective-permute-start | bytes 5308424 | tf_op jit(solution)/shard_map/ppermute | solution.py:361
  602.3 19.5 %collective-permute-start.8 = (bf16[2,768,768]{2,1,0:T(8,128)(2,1)}, bf16[2,768,768]{2,1,0:T(8,128)(2,1)}, u32[]{:S(2)}, u32[]{:S(2)}) collective-permute-start(bf16[2,768,768]{2,1,0:T(8,128)(2,1)} %bitcast.642), channel_id=1, source_target_pairs={{0,1},{1,0},{2,3},{3,2},{4,5},{5,4},{6,7},{7,6},{8,9},{9,8},{10,11... | collective-permute-start | bytes 7077896 | tf_op jit(solution)/shard_map/ppermute | solution.py:361
  603.7 8.4 collective-permute-start.6
  604.9 4.7 collective-permute-start.13
  609.6 16.3 %collective-permute-start.19 = (bf16[192,192]{1,0:T(8,128)(2,1)S(1)}, bf16[192,192]{1,0:T(8,128)(2,1)S(1)}, u32[]{:S(2)}, u32[]{:S(2)}) collective-permute-start(bf16[192,192]{1,0:T(8,128)(2,1)S(1)} %dynamic-slice_bitcast_fusion.9), channel_id=1, source_target_pairs={{0,2},{1,3},{2,0},{3,1},{4,6},{5,7},{6,4},{7,5},{8,10},{9,11},{10,... | collective-permute-start | bytes 221192 | tf_op jit(solution)/shard_map/ppermute | solution.py:364
  611.8 225.1 %all-reduce.8.cloned.1.call-start = ((), (), s32[]{:S(2)}) async-start(), calls=%async_computation.1 | async-start | bytes 7471104 | tf_op jit(solution)/shard_map/psum | solution.py:365
  612.1 15.0 %collective-permute-start.17 = (bf16[192,192]{1,0:T(8,128)(2,1)S(1)}, bf16[192,192]{1,0:T(8,128)(2,1)S(1)}, u32[]{:S(2)}, u32[]{:S(2)}) collective-permute-start(bf16[192,192]{1,0:T(8,128)(2,1)S(1)} %dynamic-slice_bitcast_fusion.10), channel_id=1, source_target_pairs={{0,2},{1,3},{2,0},{3,1},{4,6},{5,7},{6,4},{7,5},{8,10},{9,11},{10,... | collective-permute-start | bytes 221192 | tf_op jit(solution)/shard_map/ppermute | solution.py:364
  614.1 13.7 %collective-permute-start.7 = (bf16[192,768]{1,0:T(8,128)(2,1)S(1)}, bf16[192,768]{1,0:T(8,128)(2,1)S(1)}, u32[]{:S(2)}, u32[]{:S(2)}) collective-permute-start(bf16[192,768]{1,0:T(8,128)(2,1)S(1)} %dynamic-slice_bitcast_fusion.6), channel_id=1, source_target_pairs={{0,2},{1,3},{2,0},{3,1},{4,6},{5,7},{6,4},{7,5},{8,10},{9,11},{10,... | collective-permute-start | bytes 884744 | tf_op jit(solution)/shard_map/ppermute | solution.py:364
  618.3 24.8 %collective-permute-start.5 = (bf16[576,768]{1,0:T(8,128)(2,1)S(1)}, bf16[576,768]{1,0:T(8,128)(2,1)S(1)}, u32[]{:S(2)}, u32[]{:S(2)}) collective-permute-start(bf16[576,768]{1,0:T(8,128)(2,1)S(1)} %dynamic-slice_bitcast_fusion.4), channel_id=1, source_target_pairs={{0,2},{1,3},{2,0},{3,1},{4,6},{5,7},{6,4},{7,5},{8,10},{9,11},{10,... | collective-permute-start | bytes 2654216 | tf_op jit(solution)/shard_map/ppermute | solution.py:364
  621.8 46.5 %collective-permute-start.11 = (bf16[768,768]{1,0:T(8,128)(2,1)S(1)}, bf16[768,768]{1,0:T(8,128)(2,1)S(1)}, u32[]{:S(2)}, u32[]{:S(2)}) collective-permute-start(bf16[768,768]{1,0:T(8,128)(2,1)S(1)} %dynamic-slice_bitcast_fusion.2), channel_id=1, source_target_pairs={{0,2},{1,3},{2,0},{3,1},{4,6},{5,7},{6,4},{7,5},{8,10},{9,11},{10,... | collective-permute-start | bytes 3538952 | tf_op jit(solution)/shard_map/ppermute | solution.py:364
  625.9 66.7 %collective-permute-start.9 = (bf16[768,768]{1,0:T(8,128)(2,1)S(1)}, bf16[768,768]{1,0:T(8,128)(2,1)S(1)}, u32[]{:S(2)}, u32[]{:S(2)}) collective-permute-start(bf16[768,768]{1,0:T(8,128)(2,1)S(1)} %dynamic-slice_bitcast_fusion.3), channel_id=1, source_target_pairs={{0,2},{1,3},{2,0},{3,1},{4,6},{5,7},{6,4},{7,5},{8,10},{9,11},{10,... | collective-permute-start | bytes 3538952 | tf_op jit(solution)/shard_map/ppermute | solution.py:364
  (69 other events, 821.0 us)
Sparse Core Ops, SparseCore 0:
  611.9 33.7 all-reduce.5
  694.2 142.6 all-reduce.7

commit v2 on v1

--- a/solution.py
+++ b/solution.py
@@ -1,5 +1,6 @@
 import functools
 import math
+import typing
 
 import jax
 import jax.numpy as jnp
@@ -56,12 +57,6 @@
     length = sources[0][0].shape[1]
     greet(section, t, sections, tensors, ({"dp": mate},))
 
-    def rows(ref, i, which):
-        count = ref.shape[1] // 2
-        if not shared[i]:
-            return ref
-        return ref.at[:, pl.ds(pl.multiple_of(which * count, 16), count)]
-
     def part(ref, i, slot, which):
         if not shared[i]:
             return ref.at[slot]
@@ -78,13 +73,12 @@
         start = pl.multiple_of(index * length, length)
         return pages[a].at[pl.ds(start, length)] if a == 0 else pages[a].at[:, pl.ds(start, length)]
 
-    def over_pages(act):
-        for g in range(sections):
-            for j in range(2):
-                target = 2 * j + section
-                here = (section == g) & (t == target)
-                for a in range(2):
-                    act(g, j, a, target, here)
+    def over_pages(g, act):
+        for j in range(2):
+            target = 2 * j + section
+            here = (section == g) & (t == target)
+            for a in range(2):
+                act(g, j, a, target, here)
 
     def page_start(g, j, a, target, here):
         src, dst = sources[g][a].at[j], token_slot(a, t)
@@ -107,7 +101,7 @@
                 {"section": g, "tensor": target},
             ).wait_send()
 
-    over_pages(page_start)
+    over_pages(0, page_start)
 
     def to_partner(i):
         return remote(
@@ -134,15 +128,19 @@
     def keep(i):
         return pltpu.make_async_copy(weights[i], full[i].at[t], own_sem.at[i])
 
+    to_partner(0).start()
+    to_partner(1).start()
     for i in range(n_weights):
-        to_partner(i).start()
         to_sibling(i).start()
         keep(i).start()
     for i in range(n_weights):
-        to_partner(i).wait_recv()
-        on_first(i).start()
+        to_partner(i).wait()
+        if i + 2 < n_weights:
+            to_partner(i + 2).start()
         if shared[i]:
             to_mate(i).start()
+        on_first(i).start()
+    over_pages(1, page_start)
     for i in range(n_weights):
         if shared[i]:
             to_mate(i).wait_recv()
@@ -150,12 +148,12 @@
     for i in range(n_weights):
         keep(i).wait()
         to_sibling(i).wait()
-        to_partner(i).wait_send()
         on_first(i).wait()
         if shared[i]:
             to_mate(i).wait_send()
             on_second(i).wait()
-    over_pages(page_sent)
+    for g in range(sections):
+        over_pages(g, page_sent)
     for a in range(2):
         for q in range(tensors):
             slot = token_slot(a, q)
@@ -255,96 +253,372 @@
     )(text, layout)
 
 
-def norm_forward(summed, gain, offset):
-    center = summed - jnp.mean(summed, axis=-1, keepdims=True)
+GELU_P = 0.3275911
+GELU_A = (0.254829592, -0.284496736, 1.421413741, -1.453152027, 1.061405429)
+NN = (((1,), (0,)), ((), ()))
+NT = (((1,), (1,)), ((), ()))
+SCALES = (1.0 / math.sqrt(HEAD_TEXT), 1.0 / math.sqrt(HEAD_LAYOUT))
+SIZES = (HEAD_TEXT, HEAD_LAYOUT)
+ROWS = 128
+
+
+class Weights(typing.NamedTuple):
+    project: typing.Any
+    outward: typing.Any
+    upward: typing.Any
+    downward: typing.Any
+
+
+class Kept(typing.NamedTuple):
+    qkv: typing.Any
+    ctx: typing.Any
+    n1: typing.Any
+    r1: typing.Any
+    low: typing.Any
+    act: typing.Any
+    slope: typing.Any
+    n2: typing.Any
+    r2: typing.Any
+
+
+class Needed(typing.NamedTuple):
+    g: typing.Any
+    n2: typing.Any
+    r2: typing.Any
+    downward: typing.Any
+    slope: typing.Any
+    upward: typing.Any
+    n1: typing.Any
+    r1: typing.Any
+    outward: typing.Any
+    qkv: typing.Any
+    project: typing.Any
+
+
+class Back(typing.NamedTuple):
+    dx: typing.Any
+    dqkv: typing.Any
+    gf: typing.Any
+    dpre: typing.Any
+    ga: typing.Any
+
+
+def dot(a, b, dims=NN):
+    return lax.dot_general(a, b, dims, preferred_element_type=F32)
+
+
+def gelu_pair(u):
+    t = 1.0 / (1.0 + (GELU_P / math.sqrt(2.0)) * jnp.abs(u))
+    e = jnp.exp(-0.5 * (u * u))
+    a1, a2, a3, a4, a5 = (0.5 * a for a in GELU_A)
+    tail = ((((a5 * t + a4) * t + a3) * t + a2) * t + a1) * t * e
+    cdf = jnp.where(u >= 0, 1.0 - tail, tail)
+    return u * cdf, cdf + u * e * (1.0 / math.sqrt(2.0 * math.pi))
+
+
+def norm_rows(z, gain, offset):
+    center = z - jnp.mean(z, axis=-1, keepdims=True)
     inverse = lax.rsqrt(jnp.mean(center * center, axis=-1, keepdims=True) + EPSILON)
     normed = center * inverse
-    return (normed * gain + offset, normed, inverse)
-
-
-def norm_backward(upstream, normed, inverse, gain):
-    scaled = upstream * gain
-    mean_scaled = jnp.mean(scaled, axis=-1, keepdims=True)
-    mean_product = jnp.mean(scaled * normed, axis=-1, keepdims=True)
-    downstream = inverse * (scaled - mean_scaled - normed * mean_product)
-    return (downstream, jnp.sum(upstream * normed, axis=0), jnp.sum(upstream, axis=0))
-
-
-def activation(values):
-    return jax.nn.gelu(values, approximate=False)
+    return normed * gain + offset, normed, inverse
+
+
+def norm_rows_back(g, n, r, gain):
+    t = g * gain
+    return r * (t - jnp.mean(t, axis=-1, keepdims=True) - n * jnp.mean(t * n, axis=-1, keepdims=True))
+
+
+class Staged:
+    def __init__(self, tree, hbm, vmem, sem, inward):
+        self.tree, self.vmem = tree, list(vmem)
+        pairs = zip(hbm, vmem) if inward else zip(vmem, hbm)
+        self.copies = [pltpu.make_async_copy(a, b, sem.at[i]) for i, (a, b) in enumerate(pairs)]
+
+    def refs(self):
+        return jax.tree.unflatten(self.tree, self.vmem)
+
+    def parts(self):
+        return jax.tree.unflatten(self.tree, self.copies)
+
+    def start(self):
+        for copy in self.copies:
+            copy.start()
+
+    def wait(self):
+        for copy in self.copies:
+            copy.wait()
+
+
+def start(*copies):
+    for copy in copies:
+        copy.start()
+
+
+def wait(*copies):
+    for copy in copies:
+        copy.wait()
+
+
+def head_rows(stacks, slot, kind, local, scales=None):
+    rows = []
+    for b in range(2):
+        first = kind * (stacks[b].shape[1] // 3) + local * SIZES[b]
+        piece = stacks[b][slot, first : first + SIZES[b], :]
+        rows.append(piece if scales is None else piece * BF(scales[b]))
+    rows.append(jnp.zeros((128 - sum(SIZES), rows[0].shape[1]), BF))
+    return jnp.concatenate(rows, axis=0)
+
+
+def put_head(stacks, slot, kind, local, b, value):
+    first = kind * (stacks[b].shape[1] // 3) + local * SIZES[b]
+    stacks[b][slot, first : first + SIZES[b], :] = value.astype(BF)
+
+
+def forward_kernel(in_tree, out_tree, *refs):
+    n_in, n_out = in_tree.num_leaves, out_tree.num_leaves
+    hbm_in, (valid, *norms) = refs[:n_in], refs[n_in : n_in + 5]
+    hbm_out = refs[n_in + 5 : n_in + 5 + n_out]
+    rest = refs[n_in + 5 + n_out :]
+    (*nats, total_t, total_l, in_sem, out_sem) = rest[n_in + n_out :]
+    incoming = Staged(in_tree, hbm_in, rest[:n_in], in_sem, True)
+    outgoing = Staged(out_tree, hbm_out, rest[n_in : n_in + n_out], out_sem, False)
+    x, weights = incoming.refs()
+    x_in, weights_in = incoming.parts()
+    y, probs_out, kept = outgoing.refs()
+    y_out, probs_copy, kept_out = outgoing.parts()
+    slots, length = weights[0].project.shape[0], x[0].shape[0]
+    local_heads = weights[0].project.shape[1] // (3 * HEAD_TEXT)
+    incoming.start()
+    wait(*x_in, weights_in[0].project, weights_in[1].project)
+    qkv = (kept[0].qkv, kept[1].qkv)
+
+    @pl.loop(0, slots)
+    def _(t):
+        for b in range(2):
+            qkv[b][t] = dot(weights[b].project[t], x[b][...], NT).astype(BF)
+
+    start(kept_out[0].qkv, kept_out[1].qkv)
+    key_mask = valid[...] > 0
+
+    @pl.loop(0, slots)
+    def _(t):
+        for local in range(local_heads):
+            q = head_rows(qkv, t, 0, local, SCALES).T
+            scores = jnp.where(key_mask, dot(q, head_rows(qkv, t, 1, local)), NEGATIVE)
+            raised = jnp.exp(scores - jnp.max(scores, axis=-1, keepdims=True))
+            probs = (raised * (1.0 / jnp.sum(raised, axis=-1, keepdims=True))).astype(BF)
+            probs_out[t, local] = probs
+            ctx = dot(head_rows(qkv, t, 2, local), probs, NT).astype(BF)
+            kept[0].ctx[t, local * HEAD_TEXT : (local + 1) * HEAD_TEXT, :] = ctx[:HEAD_TEXT]
+            kept[1].ctx[t, local * HEAD_LAYOUT : (local + 1) * HEAD_LAYOUT, :] = ctx[
+                HEAD_TEXT : HEAD_TEXT + HEAD_LAYOUT
+            ]
+
+    start(probs_copy, kept_out[0].ctx, kept_out[1].ctx)
+    for b, total in enumerate((total_t, total_l)):
+        gains, biases = norms[2 * b : 2 * b + 2]
+        width = x[b].shape[1]
+        hidden, fed = total.at[0], total.at[1]
+        own, own_out, nat = kept[b], kept_out[b], nats[b]
+        nat[...] = own.ctx[...].reshape(width, length).T
+        wait(weights_in[b].outward)
+        wide = weights[b].outward[...].reshape(width, width)
+        for c in range(0, length, ROWS):
+            rows = slice(c, c + ROWS)
+            h, n, r = norm_rows(x[b][rows].astype(F32) + dot(nat[rows], wide), gains[0:1], biases[0:1])
+            hidden[rows] = h
+            own.n1[rows] = n
+            own.r1[rows] = r
+            own.low[rows] = h.astype(BF)
+        start(own_out.n1, own_out.r1, own_out.low)
+        wait(weights_in[b].upward, weights_in[b].downward)
+        fed[...] = jnp.zeros((length, width), F32)
+
+        @pl.loop(0, slots)
+        def _(t):
+            for c in range(0, length, 2 * ROWS):
+                rows = slice(c, c + 2 * ROWS)
+                act, slope = gelu_pair(dot(own.low[rows], weights[b].upward[t]))
+                act = act.astype(BF)
+                own.act[t, rows] = act
+                own.slope[t, rows] = slope.astype(BF)
+                fed[rows] += dot(act, weights[b].downward[t])
+
+        start(own_out.act, own_out.slope)
+        for c in range(0, length, ROWS):
+            rows = slice(c, c + ROWS)
+            out, n, r = norm_rows(hidden[rows] + fed[rows], gains[1:2], biases[1:2])
+            y[b][rows] = out.astype(BF)
+            own.n2[rows] = n
+            own.r2[rows] = r
+        start(y_out[b], own_out.n2, own_out.r2)
+    outgoing.wait()
+
+
+def vmem_like(tree):
+    return [pltpu.VMEM(s.shape, s.dtype) for s in jax.tree.leaves(tree)]
+
+
+VMEM = pl.BlockSpec(memory_space=pltpu.VMEM)
+BIG = pltpu.CompilerParams(vmem_limit_bytes=60 << 20)
+
+
+def shape(dims, dtype=BF):
+    return jax.ShapeDtypeStruct(tuple(dims), dtype)
+
+
+def layer_forward(rows, weights, norms, valid):
+    length = rows[0].shape[0]
+    slots, local_heads = weights[0].project.shape[0], weights[0].project.shape[1] // (3 * HEAD_TEXT)
+    kept = []
+    for x, w in zip(rows, weights):
+        units, column = shape((slots, length, w.upward.shape[2])), shape((length, 1), F32)
+        kept.append(Kept(
+            qkv=shape((slots, w.project.shape[1], length)), ctx=shape((slots, w.outward.shape[1], length)),
+            n1=shape(x.shape, F32), r1=column, low=shape(x.shape), act=units, slope=units,
+            n2=shape(x.shape, F32), r2=column,
+        ))
+    outs = (tuple(shape(x.shape) for x in rows), shape((slots, local_heads, length, length)), tuple(kept))
+    flat_out, out_tree = jax.tree.flatten(outs)
+    flat_in, in_tree = jax.tree.flatten((rows, weights))
+    small = (valid.astype(F32)[None], *norms[0], *norms[1])
+    results = pl.pallas_call(
+        functools.partial(forward_kernel, in_tree, out_tree),
+        out_shape=flat_out,
+        in_specs=[ANY] * len(flat_in) + [VMEM] * len(small),
+        out_specs=[ANY] * len(flat_out),
+        scratch_shapes=vmem_like(flat_in) + vmem_like(flat_out)
+        + [pltpu.VMEM(x.shape, BF) for x in rows]
+        + [pltpu.VMEM((2,) + x.shape, F32) for x in rows]
+        + [pltpu.SemaphoreType.DMA((len(flat_in),)), pltpu.SemaphoreType.DMA((len(flat_out),))],
+        compiler_params=BIG,
+        name="layer_forward",
+    )(*flat_in, *small)
+    ys, probs, kept = jax.tree.unflatten(out_tree, results)
+    return ys, (probs, kept)
+
+
+def backward_kernel(in_tree, out_tree, *refs):
+    n_in, n_out = in_tree.num_leaves, out_tree.num_leaves
+    hbm_in, gains = refs[:n_in], refs[n_in : n_in + 2]
+    hbm_out = refs[n_in + 2 : n_in + 2 + n_out]
+    norm_sums = refs[n_in + 2 + n_out : n_in + 4 + n_out]
+    rest = refs[n_in + 4 + n_out :]
+    dctx, dz, (in_sem, out_sem) = rest[n_in + n_out :][0:2], rest[n_in + n_out :][2:4], rest[n_in + n_out :][4:]
+    incoming = Staged(in_tree, hbm_in, rest[:n_in], in_sem, True)
+    outgoing = Staged(out_tree, hbm_out, rest[n_in : n_in + n_out], out_sem, False)
+    needed, probs_in = incoming.refs()
+    needed_in, probs_copy = incoming.parts()
+    back, back_out = outgoing.refs(), outgoing.parts()
+    slots, length = needed[0].project.shape[0], needed[0].g.shape[0]
+    local_heads = needed[0].project.shape[1] // (3 * HEAD_TEXT)
+    incoming.start()
+    for b in range(2):
+        own, own_in, res, res_out, gain, sums = needed[b], needed_in[b], back[b], back_out[b], gains[b], norm_sums[b]
+        wait(own_in.g, own_in.n2, own_in.r2)
+        sums[...] = jnp.zeros(sums.shape, F32)
+        for c in range(0, length, ROWS):
+            rows = slice(c, c + ROWS)
+            g, n = own.g[rows].astype(F32), own.n2[rows]
+            low = norm_rows_back(g, n, own.r2[rows], gain[1:2])
+            dz[b][rows] = low
+            res.gf[rows] = low.astype(BF)
+            sums[1:2] += jnp.sum(g * n, axis=0, keepdims=True)
+            sums[3:4] += jnp.sum(g, axis=0, keepdims=True)
+        start(res_out.gf)
+        wait(own_in.downward, own_in.slope, own_in.upward)
+
+        @pl.loop(0, slots)
+        def _(t):
+            for c in range(0, length, 2 * ROWS):
+                rows = slice(c, c + 2 * ROWS)
+                d_act = dot(res.gf[rows], own.downward[t], NT)
+                d_pre = (d_act * own.slope[t, rows].astype(F32)).astype(BF)
+                res.dpre[t, rows] = d_pre
+                dz[b][rows] += dot(d_pre, own.upward[t], NT)
+
+        start(res_out.dpre)
+        wait(own_in.n1, own_in.r1)
+        for c in range(0, length, ROWS):
+            rows = slice(c, c + ROWS)
+            g, n = dz[b][rows], own.n1[rows]
+            low = norm_rows_back(g, n, own.r1[rows], gain[0:1])
+            dz[b][rows] = low
+            res.ga[rows] = low.astype(BF)
+            sums[0:1] += jnp.sum(g * n, axis=0, keepdims=True)
+            sums[2:3] += jnp.sum(g, axis=0, keepdims=True)
+        start(res_out.ga)
+        wait(own_in.outward)
+        for t in range(slots):
+            dctx[b][t] = dot(own.outward[t], res.ga[...], NT).astype(BF)
+    wait(needed_in[0].qkv, needed_in[1].qkv, probs_copy)
+    qkv, dqkv = (needed[0].qkv, needed[1].qkv), (back[0].dqkv, back[1].dqkv)
+    text_rows, layout_rows = slice(0, HEAD_TEXT), slice(HEAD_TEXT, HEAD_TEXT + HEAD_LAYOUT)
+
+    @pl.loop(0, slots)
+    def _(t):
+        for local in range(local_heads):
+            dcT = jnp.concatenate(
+                [dctx[b][t, local * SIZES[b] : (local + 1) * SIZES[b], :] for b in range(2)]
+                + [jnp.zeros((128 - sum(SIZES), length), BF)], axis=0,
+            )
+            dc = dcT.T
+            lane = lax.broadcasted_iota(jnp.int32, dc.shape, 1)
+            dc_layout = jnp.where(lane >= HEAD_TEXT, dc, jnp.zeros_like(dc))
+            qT, kT, vT = (head_rows(qkv, t, kind, local, SCALES if kind == 0 else None) for kind in range(3))
+            low = probs_in[t, local]
+            probs = low.astype(F32)
+            both = dot(dc, vT)
+            ds_both = (probs * (both - jnp.sum(probs * both, axis=-1, keepdims=True))).astype(BF)
+            single = dot(dc_layout, vT)
+            ds_layout = (probs * (single - jnp.sum(probs * single, axis=-1, keepdims=True))).astype(BF)
+            dvT = dot(dcT, low)
+            put_head(dqkv, t, 2, local, 0, dvT[text_rows])
+            put_head(dqkv, t, 2, local, 1, dvT[layout_rows])
+            put_head(dqkv, t, 0, local, 0, dot(kT[text_rows], ds_both, NT) * SCALES[0])
+            put_head(dqkv, t, 1, local, 0, dot(qT[text_rows], ds_both))
+            put_head(dqkv, t, 0, local, 1, dot(kT[layout_rows], ds_layout, NT) * SCALES[1])
+            put_head(dqkv, t, 1, local, 1, dot(qT[layout_rows], ds_layout))
+
+    start(back_out[0].dqkv, back_out[1].dqkv)
+    for b in range(2):
+        wait(needed_in[b].project)
+        for t in range(slots):
+            dz[b][...] += dot(dqkv[b][t].T, needed[b].project[t])
+        back[b].dx[...] = dz[b][...].astype(BF)
+        start(back_out[b].dx)
+    outgoing.wait()
+
+
+def layer_backward(saved, grads, weights, norms):
+    probs, kept = saved
+    needed, back = [], []
+    for g, k, w in zip(grads, kept, weights):
+        needed.append(Needed(
+            g=g, n2=k.n2, r2=k.r2, downward=w.downward, slope=k.slope, upward=w.upward, n1=k.n1, r1=k.r1,
+            outward=w.outward, qkv=k.qkv, project=w.project,
+        ))
+        rows = shape(g.shape)
+        back.append(Back(dx=rows, dqkv=shape(k.qkv.shape), gf=rows, dpre=shape(k.slope.shape), ga=rows))
+    flat_in, in_tree = jax.tree.flatten((tuple(needed), probs))
+    flat_out, out_tree = jax.tree.flatten(tuple(back))
+    results = pl.pallas_call(
+        functools.partial(backward_kernel, in_tree, out_tree),
+        out_shape=flat_out + [shape((4, g.shape[1]), F32) for g in grads],
+        in_specs=[ANY] * len(flat_in) + [VMEM] * 2,
+        out_specs=[ANY] * len(flat_out) + [VMEM] * 2,
+        scratch_shapes=vmem_like(flat_in) + vmem_like(flat_out)
+        + [pltpu.VMEM(k.ctx.shape, BF) for k in kept]
+        + [pltpu.VMEM(g.shape, F32) for g in grads]
+        + [pltpu.SemaphoreType.DMA((len(flat_in),)), pltpu.SemaphoreType.DMA((len(flat_out),))],
+        compiler_params=BIG,
+        name="layer_backward",
+    )(*flat_in, norms[0][0], norms[1][0])
+    return jax.tree.unflatten(out_tree, results[:-2]), tuple(results[-2:])
 
 
 def mm(spec, a, b):
     return jnp.einsum(spec, a, b, preferred_element_type=F32)
-
-
-def layer_forward(rows, weights, norms, valid):
-    heads = []
-    for b in range(2):
-        qkv = mm("ld,tnd->ltn", rows[b], weights[b][0]).astype(BF)
-        heads.append(qkv.reshape(qkv.shape[0], qkv.shape[1], 3, -1, (HEAD_TEXT, HEAD_LAYOUT)[b]))
-    scores = mm("qthd,kthd->thqk", heads[0][:, :, 0], heads[0][:, :, 1]) * (1.0 / math.sqrt(HEAD_TEXT))
-    scores = scores + mm("qthd,kthd->thqk", heads[1][:, :, 0], heads[1][:, :, 1]) * (
-        1.0 / math.sqrt(HEAD_LAYOUT)
-    )
-    scores = jnp.where(valid[None, None, None, :], scores, NEGATIVE)
-    highest = jnp.max(scores, axis=-1, keepdims=True)
-    raised = jnp.exp(scores - highest)
-    probs = (raised / jnp.sum(raised, axis=-1, keepdims=True)).astype(BF)
-    outs, kept = [], []
-    for b in range(2):
-        gains, biases = norms[b]
-        context = mm("thqk,kthd->qthd", probs, heads[b][:, :, 2]).astype(BF)
-        context = context.reshape(context.shape[0], context.shape[1], -1)
-        attended = mm("ltn,tnd->ld", context, weights[b][1])
-        hidden, n1, r1 = norm_forward(rows[b].astype(F32) + attended, gains[0], biases[0])
-        low = hidden.astype(BF)
-        pre = mm("ld,tdn->ltn", low, weights[b][2])
-        active = activation(pre).astype(BF)
-        fed = mm("ltn,tnd->ld", active, weights[b][3])
-        out, n2, r2 = norm_forward(hidden + fed, gains[1], biases[1])
-        outs.append(out.astype(BF))
-        kept.append((context, n1, r1, low, pre, active, n2, r2))
-    return tuple(outs), (tuple(heads), probs, tuple(kept))
-
-
-def layer_backward(saved, grads, weights, norms):
-    heads, probs, kept = saved
-    probs_f = probs.astype(F32)
-    norm_grads, operands, dz_ones, score_grads, context_grads = [], [], [], [], []
-    for b in range(2):
-        gains, biases = norms[b]
-        context, n1, r1, low, pre, active, n2, r2 = kept[b]
-        dz_two, g2, b2 = norm_backward(grads[b].astype(F32), n2, r2, gains[1])
-        gf = dz_two.astype(BF)
-        d_active = mm("ld,tnd->ltn", gf, weights[b][3])
-        d_pre = jax.vjp(activation, pre)[1](d_active)[0].astype(BF)
-        d_hidden = dz_two + mm("ltn,tdn->ld", d_pre, weights[b][2])
-        dz_one, g1, b1 = norm_backward(d_hidden, n1, r1, gains[0])
-        ga = dz_one.astype(BF)
-        d_context = mm("ld,tnd->ltn", ga, weights[b][1]).astype(BF)
-        d_context = d_context.reshape(heads[b][:, :, 2].shape)
-        d_probs = mm("qthd,kthd->thqk", d_context, heads[b][:, :, 2])
-        inner = jnp.sum(probs_f * d_probs, axis=-1, keepdims=True)
-        score_grads.append((probs_f * (d_probs - inner)).astype(BF))
-        context_grads.append(d_context)
-        dz_ones.append(dz_one)
-        norm_grads.append((jnp.stack([g1, g2]), jnp.stack([b1, b2])))
-        operands.append([gf, d_pre, ga])
-    total = (score_grads[0].astype(F32) + score_grads[1].astype(F32)).astype(BF)
-    reaching = (total, score_grads[1])
-    downs, out_operands = [], []
-    for b in range(2):
-        scale = 1.0 / math.sqrt((HEAD_TEXT, HEAD_LAYOUT)[b])
-        dq = (mm("thqk,kthd->qthd", reaching[b], heads[b][:, :, 1]) * scale).astype(BF)
-        dk = (mm("thqk,qthd->kthd", reaching[b], heads[b][:, :, 0]) * scale).astype(BF)
-        dv = mm("thqk,qthd->kthd", probs, context_grads[b]).astype(BF)
-        stacked = jnp.stack([dq, dk, dv], axis=2)
-        stacked = stacked.reshape(stacked.shape[0], stacked.shape[1], -1)
-        down = dz_ones[b] + mm("ltn,tnd->ld", stacked, weights[b][0])
-        downs.append(down.astype(BF))
-        out_operands.append((stacked, *operands[b]))
-    return tuple(downs), tuple(out_operands), tuple(norm_grads)
 
 
 def zeros_like_tree(shapes):
@@ -408,7 +682,7 @@
     text_page, layout_page, full = fetch(
         mesh, embedded, flipped(layout_input), text_cotangent[0], flipped(layout_cotangent), shards
     )
-    weights = (full[0:4], full[4:8])
+    weights = (Weights(*full[0:4]), Weights(*full[4:8]))
     norms = ((text_gains[0], text_biases[0]), (layout_gains[0], layout_biases[0]))
     counts = page_counts[micro, page]
     positions = jnp.arange(pad_mask.shape[2], dtype=jnp.int32)
@@ -428,21 +702,20 @@
 
     back_shapes = jax.eval_shape(back, arrived)
     first = lax.cond(section == 1, back, lambda grads: zeros_like_tree(back_shapes), arrived)
-    hopped = tuple(lax.ppermute(block, "section", [(1, 0)]) for block in first[0])
-    downs, operands, norm_grads = lax.cond(
+    hopped = tuple(lax.ppermute(res.dx, "section", [(1, 0)]) for res in first[0])
+    back_results, norm_grads = lax.cond(
         section == 0, lambda old, got: back(got), lambda old, got: old, first, hopped
     )
-    _, _, kept = saved
-    grads = []
-    for b in range(2):
-        stacked, gf, d_pre, ga = operands[b]
-        context, n1, r1, low, pre, active, n2, r2 = kept[b]
-        grads.append((
-            mm("ltn,ld->tnd", stacked, rows[b]).astype(BF),
-            mm("ltn,ld->tnd", context, ga).astype(BF),
-            mm("ld,ltn->tdn", low, d_pre).astype(BF),
-            mm("ltn,ld->tnd", active, gf).astype(BF),
-        ))
+    downs = tuple(res.dx for res in back_results)
+    grads = [
+        (
+            mm("tnl,ld->tnd", res.dqkv, rows[b]).astype(BF),
+            mm("tnl,ld->tnd", saved[1][b].ctx, res.ga).astype(BF),
+            mm("ld,tln->tdn", saved[1][b].low, res.dpre).astype(BF),
+            mm("tln,ld->tnd", saved[1][b].act, res.gf).astype(BF),
+        )
+        for b, res in enumerate(back_results)
+    ]
     final = tuple(jnp.where(section == 0, d, o) for d, o in zip(downs, outs))
     text_out, layout_out, text_grad, layout_grad = give_back(mesh, final[0], final[1].T)
     summed = [[reduce_shard(g, t, tensors) for g in per_stream] for per_stream in grads]
@@ -452,7 +725,7 @@
     lang_grad = (groups == own_group).astype(F32)[:, None] * page_sum[None, :]
     pick = (jnp.arange(2, dtype=jnp.int32) == section).astype(F32)[:, None, None]
     small = lax.psum(
-        tuple(pick * member[None] for pair in norm_grads for member in pair) + (lang_grad,),
+        tuple(pick * member[None] for sums in norm_grads for member in (sums[0:2], sums[2:4])) + (lang_grad,),
         ("section", "dp", "tensor"),
     )
 

time: 862 us -> 626 us (0.73)
  matrix products: 170 us -> 20.4 us
  waiting for transfers between devices: 351 us -> 232 us
  Pallas kernels: 129 us -> 206 us
  other arithmetic: 72 us -> 38.3 us
  loops' own time: 12.7 us -> 0.98 us
    dot_general x33 -> x8, matrix products: 157 us -> 20.2 us  [mm(): return jnp.einsum(spec, a, b, preferred_element_type=F32)]
    ppermute x2, waiting for transfers between devices: 195 us -> 79 us  [per_device(): lax.ppermute(res.dx, 'section', [(1, 0)])]
    pallas_call x0 -> x2, Pallas kernels: none -> 66.1 us  [the longest x1 33.8 us: layer_forward(): pl.pallas_call(functools.partial(forward_kernel, in_tree, out_tree), out_...]
    convert_element_type x11 -> x0, other arithmetic: 27.9 us -> none  [the longest x1 9.15 us: layer_forward(): probs = (raised / jnp.sum(raised, axis=-1, keepdims=True)).astype(BF)]
    pallas_call x1, Pallas kernels: 116 us -> 127 us  [fetch(): pl.pallas_call(functools.partial(fetch_kernel, sections, tensors, dp, sha...]
    sub x1 -> x0, matrix products: 11.1 us -> none  [layer_forward(): raised = jnp.exp(scores - highest)]
  transfers between devices with their start and end apart: 22 -> 22, of which waited for: 7 -> 7; matrix products, arithmetic and copies ran while one was open for 8% -> 10% of each run, Pallas kernels for 1% -> 2%
where the time goes in v2:
time: 626 us; the launch traced here: 616 us
  waiting for transfers between devices  232 us (37%)
  Pallas kernels  206 us (33%)
  blocking collectives  46.8 us (7%)
  local copies, waits for them, and re-layouts  39.4 us (6%)
  other arithmetic  38.3 us (6%)
  matrix products  20.4 us (3%)
  starting transfers between devices  17.3 us (3%)
  between operations  15.1 us (2%)
    pallas_call x1, Pallas kernels, fetch(): pl.pallas_call(functools.partial(fetch_kernel, sections, tensors, dp, sha...  127 us
    ppermute x2, waiting for transfers between devices, per_device(): lax.ppermute(res.dx, 'section', [(1, 0)])  79 us
    psum x2, waiting for transfers between devices, reduce_shard(): return lax.psum(summed, 'dp').astype(F32)  75.3 us
    ppermute x8, waiting for transfers between devices, reduce_shard(): lax.ppermute(theirs, 'tensor', partner).astype(F32)  63 us
    psum x1, blocking collectives, per_device(): lax.psum(tuple((pick * member[None] for sums in norm_grads for member in...  46.8 us
    pallas_call x1, Pallas kernels, layer_forward(): pl.pallas_call(functools.partial(forward_kernel, in_tree, out_tree), out_...  33.8 us
    pallas_call x1, Pallas kernels, layer_backward(): pl.pallas_call(functools.partial(backward_kernel, in_tree, out_tree), out...  32.3 us
    dot_general x8, matrix products, mm(): return jnp.einsum(spec, a, b, preferred_element_type=F32)  20.2 us
  transfers between devices with their start and end apart: 22, of which 7 were waited for; matrix products, arithmetic and copies ran while one was open for 10% of the time, Pallas kernels for 2%

profile of v2, /device:TPU:0, one launch (start us, length us, event | category | flops | bytes accessed | tf_op | source)
XLA Modules:
  0.0 616.3 jit_solution(12836730855693280462)
XLA Ops:
  12.6 127.4 %fetch.1 = (bf16[512,768]{1,0:T(8,128)(2,1)}, bf16[192,512]{1,0:T(8,128)(2,1)S(1)}, bf16[4,576,768]{2,1,0:T(8,128)(2,1)}, bf16[4,192,768]{2,1,0:T(8,128)(2,1)}, ...) custom-call(bf16[2,128,768]{2,1,0:T(8,128)(2,1)} %fusion.9.refs_0_, ...), custom_call_target="tpu_custom_call" | custom-call | tf_op jit(solution)/shard_map/fetch/pallas_call | solution.py:172
  140.7 36.2 %conditional.4 = (bf16[512,768]{1,0:T(8,128)(2,1)}, bf16[512,192]{1,0:T(8,128)(2,1)}, bf16[512,768]{1,0:T(8,128)(2,1)}, bf16[512,192]{1,0:T(8,128)(2,1)}, bf16[4...) conditional(s32[]{:T(128)} %convert_element_type.273, () %tuple.53, ...), branch_computations={%region_0.1_spmd, %region_1.2_spmd} | conditional | flops 512 | bytes 24977654 | solution.py:696
  142.1 33.8 %layer_forward.2 = (bf16[512,768]{1,0:T(8,128)(2,1)}, bf16[512,192]{1,0:T(8,128)(2,1)}, bf16[4,3,512,512]{3,2,1,0:T(8,128)(2,1)}, bf16[4,576,512]{2,1,0:T(8,128)...) custom-call(bf16[512,768]{1,0:T(8,128)(2,1)} %get-tuple-element.874., ...), custom_call_target="tpu_custom_call" | custom-call | tf_op jit(solution)/shard_map/cond/branch_1_fun/layer_forward/pallas_call | solution.py:485
  176.9 2.2 collective-permute-start
  181.0 14.5 %collective-permute-done.1 = bf16[512,192]{1,0:T(8,128)(2,1)} collective-permute-done((bf16[512,192]{1,0:T(8,128)(2,1)}, bf16[512,192]{1,0:T(8,128)(2,1)}, u32[]{:S(2)}, u32[]{:S(2)}) %collective-permute-start.1) | collective-permute-done | bytes 196640 | tf_op jit(solution)/shard_map/ppermute | solution.py:697
  197.5 10.9 %conditional.6 = ((bf16[512,768]{1,0:T(8,128)(2,1)}, bf16[4,576,512]{2,1,0:T(8,128)(2,1)}, bf16[512,768]{1,0:T(8,128)(2,1)}, bf16[4,512,768]{2,1,0:T(8,128)(2,1)...) conditional(s32[]{:T(128)} %convert_element_type.274, () %tuple.52, ...), branch_computations={%region_4.5_spmd, %region_5.6_spmd} | conditional | bytes 9845892 | solution.py:704
  211.0 79.0 %collective-permute-done.3 = bf16[512,192]{1,0:T(8,128)(2,1)} collective-permute-done((bf16[512,192]{1,0:T(8,128)(2,1)}, bf16[512,192]{1,0:T(8,128)(2,1)}, u32[]{:S(2)}, u32[]{:S(2)}) %collective-permute-start.3) | collective-permute-done | bytes 196640 | tf_op jit(solution)/shard_map/ppermute | solution.py:705
  290.0 32.6 %conditional.7 = ((bf16[512,768]{1,0:T(8,128)(2,1)}, bf16[4,576,512]{2,1,0:T(8,128)(2,1)}, bf16[512,768]{1,0:T(8,128)(2,1)}, bf16[4,512,768]{2,1,0:T(8,128)(2,1)...) conditional(s32[]{:T(128)} %convert_element_type.273, ...), branch_computations={%region_6.7_spmd.clone, %region_7.8_spmd.clone} | conditional | bytes 8 | solution.py:706
  290.2 32.3 %layer_backward.5 = (bf16[512,768]{1,0:T(8,128)(2,1)}, bf16[4,576,512]{2,1,0:T(8,128)(2,1)}, bf16[512,768]{1,0:T(8,128)(2,1)}, bf16[4,512,768]{2,1,0:T(8,128)(2,...) custom-call(bf16[512,768]{1,0:T(8,128)(2,1)} %get-tuple-element.773., ...), custom_call_target="tpu_custom_call" | custom-call | tf_op jit(solution)/shard_map/cond/branch_1_fun/layer_backward/pallas_call | solution.py:605
  333.4 4.5 convolution_convert_fusion
  342.1 4.0 convolution_convert_fusion.1
  350.0 3.6 convolution_convert_fusion.2
  357.3 2.4 copy.44
  359.8 2.8 copy.72
  376.8 2.4 fusion.2
  379.9 2.9 fusion
  384.6 2.2 fusion.1
  390.4 13.8 %collective-permute-done.5 = bf16[576,768]{1,0:T(8,128)(2,1)S(1)} collective-permute-done((bf16[576,768]{1,0:T(8,128)(2,1)S(1)}, bf16[576,768]{1,0:T(8,128)(2,1)S(1)}, u32[]{:S(2)}, u32[]{:S(2)}) %collective-permute-start.5) | collective-permute-done | bytes 884768 | tf_op jit(solution)/shard_map/ppermute | solution.py:638
  405.3 24.2 %collective-permute-done.11 = bf16[768,768]{1,0:T(8,128)(2,1)S(1)} collective-permute-done((bf16[768,768]{1,0:T(8,128)(2,1)S(1)}, bf16[768,768]{1,0:T(8,128)(2,1)S(1)}, u32[]{:S(2)}, u32[]{:S(2)}) %collective-permute-start.11) | collective-permute-done | bytes 1179680 | tf_op jit(solution)/shard_map/ppermute | solution.py:638
  430.8 23.0 %collective-permute-done.9 = bf16[768,768]{1,0:T(8,128)(2,1)S(1)} collective-permute-done((bf16[768,768]{1,0:T(8,128)(2,1)S(1)}, bf16[768,768]{1,0:T(8,128)(2,1)S(1)}, u32[]{:S(2)}, u32[]{:S(2)}) %collective-permute-start.9) | collective-permute-done | bytes 1179680 | tf_op jit(solution)/shard_map/ppermute | solution.py:638
  458.8 12.6 %give_back.1 = (bf16[2,128,768]{2,1,0:T(8,128)(2,1)}, bf16[2,192,128]{2,1,0:T(8,128)(2,1)}, bf16[2,128,768]{2,1,0:T(8,128)(2,1)}, bf16[2,192,128]{2,1,0:T(8,128)(2,1)}) custom-call(bf16[512,768]{1,0:T(8,128)(2,1)} %broadcast_select_fusion.text, bf16[192,512]{1,0:T(8,128)(2,1)} %select_bitcast_fusion.layout), custom_call_target="tpu_custom_call" | custom-call | tf_op jit(solution)/shard_map/give_back/pallas_call | solution.py:242
  471.8 46.8 %all-reduce = (f32[8,768]{1,0:T(8,128)}, f32[2,2,768]{2,1,0:T(2,128)S(1)}, f32[2,2,768]{2,1,0:T(2,128)S(1)}, f32[2,2,192]{2,1,0:T(2,128)S(1)}, f32[2,2,192]{2,1,0:T(2,128)S(1)}) all-reduce(f32[8,768]{1,0:T(8,128)S(1)} %broadcast_multiply_fusion, ...), channel_id=1, replica_groups=mesh['section'=2,'dp'=4,'tensor'=4] {'section','dp','tensor'}, use_global_device_ids=true, to_apply=%region_9.10 | all-reduce | flops 13824 | bytes 110592 | tf_op jit(solution)/shard_map/psum | solution.py:727
  522.7 75.3 %all-reduce.8.cloned.1.call-done = (bf16[1,768,3,192]{1,3,2,0:T(8,128)(2,1)}, bf16[1,192,768]{2,1,0:T(8,128)(2,1)}, bf16[1,768,768]{2,1,0:T(8,128)(2,1)}, bf16[1...) async-done(((bf16[1,768,3,192]{1,3,2,0:T(8,128)(2,1)}, bf16[1,192,768]{2,1,0:T(8,128)(2,1)}, bf16[1,768,768]{2,1,0:T(8,128)(2,1)}, ...) | async-done | bytes 3686416 | tf_op jit(solution)/shard_map/psum | solution.py:639
  598.0 2.9 broadcast_in_dim.94
  (188 shorter events, 89.5 us)
Async XLA Ops:
  7.2 512.6 %all-reduce.6.cloned.1.call-start = ((), (), s32[]{:S(2)}) async-start(), calls=%async_computation | async-start | bytes 196608 | tf_op jit(solution)/shard_map/psum | solution.py:639
  12.6 127.4 %copy-start.29 = (f32[1,2,768]{2,1,0:T(2,128)S(1)}, f32[1,2,768]{2,1,0:T(2,128)}, u32[]{:S(2)}) copy-start(f32[1,2,768]{2,1,0:T(2,128)} %param.41) | copy-start | bytes 18436
  12.6 127.4 %copy-start.30 = (f32[1,2,192]{2,1,0:T(2,128)S(1)}, f32[1,2,192]{2,1,0:T(2,128)}, u32[]{:S(2)}) copy-start(f32[1,2,192]{2,1,0:T(2,128)} %param.47) | copy-start | bytes 4612
  176.9 18.6 %collective-permute-start = (bf16[512,768]{1,0:T(8,128)(2,1)}, bf16[512,768]{1,0:T(8,128)(2,1)}, u32[]{:S(2)}, u32[]{:S(2)}) collective-permute-start(bf16[512,768]{1,0:T(8,128)(2,1)} %get-tuple-element.604), channel_id=1, source_target_pairs={{0,16},{1,17},{2,18},{3,19},{4,20},{5,21},{6,22},{7,23},{8,24},{9,... | collective-permute-start | bytes 2359304 | tf_op jit(solution)/shard_map/ppermute | solution.py:697
  179.0 16.5 %collective-permute-start.1 = (bf16[512,192]{1,0:T(8,128)(2,1)}, bf16[512,192]{1,0:T(8,128)(2,1)}, u32[]{:S(2)}, u32[]{:S(2)}) collective-permute-start(bf16[512,192]{1,0:T(8,128)(2,1)} %get-tuple-element.605), channel_id=1, source_target_pairs={{0,16},{1,17},{2,18},{3,19},{4,20},{5,21},{6,22},{7,23},{8,24},{9,... | collective-permute-start | bytes 589832 | tf_op jit(solution)/shard_map/ppermute | solution.py:697
  208.4 81.6 %collective-permute-start.2 = (bf16[512,768]{1,0:T(8,128)(2,1)}, bf16[512,768]{1,0:T(8,128)(2,1)}, u32[]{:S(2)}, u32[]{:S(2)}) collective-permute-start(bf16[512,768]{1,0:T(8,128)(2,1)} %get-tuple-element.619), channel_id=1, source_target_pairs={{16,0},{17,1},{18,2},{19,3},{20,4},{21,5},{22,6},{23,7},{24,8},{25... | collective-permute-start | bytes 2359304 | tf_op jit(solution)/shard_map/ppermute | solution.py:705
  209.7 80.3 %collective-permute-start.3 = (bf16[512,192]{1,0:T(8,128)(2,1)}, bf16[512,192]{1,0:T(8,128)(2,1)}, u32[]{:S(2)}, u32[]{:S(2)}) collective-permute-start(bf16[512,192]{1,0:T(8,128)(2,1)} %get-tuple-element.620), channel_id=1, source_target_pairs={{16,0},{17,1},{18,2},{19,3},{20,4},{21,5},{22,6},{23,7},{24,8},{25... | collective-permute-start | bytes 589832 | tf_op jit(solution)/shard_map/ppermute | solution.py:705
  324.7 30.2 %collective-permute-start.14 = (bf16[2,48,192]{2,1,0:T(8,128)(2,1)}, bf16[2,48,192]{2,1,0:T(8,128)(2,1)}, u32[]{:S(2)}, u32[]{:S(2)}) collective-permute-start(bf16[2,48,192]{2,1,0:T(8,128)(2,1)} %dynamic-slice_bitcast_fusion.12), channel_id=1, source_target_pairs={{0,1},{1,0},{2,3},{3,2},{4,5},{5,4},{6,7},{7,6},{8,9},{9,8},{10,11... | collective-permute-start | bytes 110600 | tf_op jit(solution)/shard_map/ppermute | solution.py:635
  326.8 36.5 %collective-permute-start.12 = (bf16[2,144,192]{2,1,0:T(8,128)(2,1)}, bf16[2,144,192]{2,1,0:T(8,128)(2,1)}, u32[]{:S(2)}, u32[]{:S(2)}) collective-permute-start(bf16[2,144,192]{2,1,0:T(8,128)(2,1)} %dynamic-slice_bitcast_fusion.8), channel_id=1, source_target_pairs={{0,1},{1,0},{2,3},{3,2},{4,5},{5,4},{6,7},{7,6},{8,9},{9,8},{10,11... | collective-permute-start | bytes 331784 | tf_op jit(solution)/shard_map/ppermute | solution.py:635
  329.9 34.9 %collective-permute-start.18 = (bf16[2,192,192]{2,1,0:T(8,128)(2,1)}, bf16[2,192,192]{2,1,0:T(8,128)(2,1)}, u32[]{:S(2)}, u32[]{:S(2)}) collective-permute-start(bf16[2,192,192]{2,1,0:T(8,128)(2,1)} %dynamic-slice_bitcast_fusion.7), channel_id=1, source_target_pairs={{0,1},{1,0},{2,3},{3,2},{4,5},{5,4},{6,7},{7,6},{8,9},{9,8},{10,11... | collective-permute-start | bytes 442376 | tf_op jit(solution)/shard_map/ppermute | solution.py:635
  332.9 33.1 %collective-permute-start.16 = (bf16[2,192,192]{2,1,0:T(8,128)(2,1)}, bf16[2,192,192]{2,1,0:T(8,128)(2,1)}, u32[]{:S(2)}, u32[]{:S(2)}) collective-permute-start(bf16[2,192,192]{2,1,0:T(8,128)(2,1)} %bitcast.88), channel_id=1, source_target_pairs={{0,1},{1,0},{2,3},{3,2},{4,5},{5,4},{6,7},{7,6},{8,9},{9,8},{10,11... | collective-permute-start | bytes 442376 | tf_op jit(solution)/shard_map/ppermute | solution.py:635
  341.4 38.0 %collective-permute-start.10 = (bf16[2,768,768]{2,1,0:T(8,128)(2,1)}, bf16[2,768,768]{2,1,0:T(8,128)(2,1)}, u32[]{:S(2)}, u32[]{:S(2)}) collective-permute-start(bf16[2,768,768]{2,1,0:T(8,128)(2,1)} %dynamic-slice_bitcast_fusion), channel_id=1, source_target_pairs={{0,1},{1,0},{2,3},{3,2},{4,5},{5,4},{6,7},{7,6},{8,9},{9,8},{10,11... | collective-permute-start | bytes 7077896 | tf_op jit(solution)/shard_map/ppermute | solution.py:635
  355.8 6.8 %collective-permute-start.15 = (bf16[48,192]{1,0:T(8,128)(2,1)S(1)}, bf16[48,192]{1,0:T(8,128)(2,1)S(1)}, u32[]{:S(2)}, u32[]{:S(2)}) collective-permute-start(bf16[48,192]{1,0:T(8,128)(2,1)S(1)} %dynamic-slice_bitcast_fusion.13), channel_id=1, source_target_pairs={{0,2},{1,3},{2,0},{3,1},{4,6},{5,7},{6,4},{7,5},{8,10},{9,11},{10,... | collective-permute-start | bytes 55304 | tf_op jit(solution)/shard_map/ppermute | solution.py:638
  362.6 12.6 %collective-permute-start.4 = (bf16[2,576,768]{2,1,0:T(8,128)(2,1)}, bf16[2,576,768]{2,1,0:T(8,128)(2,1)}, u32[]{:S(2)}, u32[]{:S(2)}) collective-permute-start(bf16[2,576,768]{2,1,0:T(8,128)(2,1)} %dynamic-slice_bitcast_fusion.1), channel_id=1, source_target_pairs={{0,1},{1,0},{2,3},{3,2},{4,5},{5,4},{6,7},{7,6},{8,9},{9,8},{10,11... | collective-permute-start | bytes 5308424 | tf_op jit(solution)/shard_map/ppermute | solution.py:635
  363.3 19.6 %collective-permute-start.8 = (bf16[2,768,768]{2,1,0:T(8,128)(2,1)}, bf16[2,768,768]{2,1,0:T(8,128)(2,1)}, u32[]{:S(2)}, u32[]{:S(2)}) collective-permute-start(bf16[2,768,768]{2,1,0:T(8,128)(2,1)} %bitcast.206), channel_id=1, source_target_pairs={{0,1},{1,0},{2,3},{3,2},{4,5},{5,4},{6,7},{7,6},{8,9},{9,8},{10,11... | collective-permute-start | bytes 7077896 | tf_op jit(solution)/shard_map/ppermute | solution.py:635
  364.8 8.4 %collective-permute-start.6 = (bf16[2,192,768]{2,1,0:T(8,128)(2,1)}, bf16[2,192,768]{2,1,0:T(8,128)(2,1)}, u32[]{:S(2)}, u32[]{:S(2)}) collective-permute-start(bf16[2,192,768]{2,1,0:T(8,128)(2,1)} %dynamic-slice_bitcast_fusion.5), channel_id=1, source_target_pairs={{0,1},{1,0},{2,3},{3,2},{4,5},{5,4},{6,7},{7,6},{8,9},{9,8},{10,11... | collective-permute-start | bytes 1769480 | tf_op jit(solution)/shard_map/ppermute | solution.py:635
  366.0 4.7 collective-permute-start.13
  370.7 16.2 %collective-permute-start.19 = (bf16[192,192]{1,0:T(8,128)(2,1)S(1)}, bf16[192,192]{1,0:T(8,128)(2,1)}, u32[]{:S(2)}, u32[]{:S(2)}) collective-permute-start(bf16[192,192]{1,0:T(8,128)(2,1)S(1)} %dynamic-slice_bitcast_fusion.9), channel_id=1, source_target_pairs={{0,2},{1,3},{2,0},{3,1},{4,6},{5,7},{6,4},{7,5},{8,10},{9,11},{10,... | collective-permute-start | bytes 221192 | tf_op jit(solution)/shard_map/ppermute | solution.py:638
  372.9 225.1 %all-reduce.8.cloned.1.call-start = ((), (), s32[]{:S(2)}) async-start(), calls=%async_computation.1 | async-start | bytes 7471104 | tf_op jit(solution)/shard_map/psum | solution.py:639
  373.2 15.7 %collective-permute-start.17 = (bf16[192,192]{1,0:T(8,128)(2,1)S(1)}, bf16[192,192]{1,0:T(8,128)(2,1)S(1)}, u32[]{:S(2)}, u32[]{:S(2)}) collective-permute-start(bf16[192,192]{1,0:T(8,128)(2,1)S(1)} %dynamic-slice_bitcast_fusion.10), channel_id=1, source_target_pairs={{0,2},{1,3},{2,0},{3,1},{4,6},{5,7},{6,4},{7,5},{8,10},{9,11},{10,... | collective-permute-start | bytes 221192 | tf_op jit(solution)/shard_map/ppermute | solution.py:638
  375.2 14.4 %collective-permute-start.7 = (bf16[192,768]{1,0:T(8,128)(2,1)S(1)}, bf16[192,768]{1,0:T(8,128)(2,1)S(1)}, u32[]{:S(2)}, u32[]{:S(2)}) collective-permute-start(bf16[192,768]{1,0:T(8,128)(2,1)S(1)} %dynamic-slice_bitcast_fusion.6), channel_id=1, source_target_pairs={{0,2},{1,3},{2,0},{3,1},{4,6},{5,7},{6,4},{7,5},{8,10},{9,11},{10,... | collective-permute-start | bytes 884744 | tf_op jit(solution)/shard_map/ppermute | solution.py:638
  379.4 24.8 %collective-permute-start.5 = (bf16[576,768]{1,0:T(8,128)(2,1)S(1)}, bf16[576,768]{1,0:T(8,128)(2,1)S(1)}, u32[]{:S(2)}, u32[]{:S(2)}) collective-permute-start(bf16[576,768]{1,0:T(8,128)(2,1)S(1)} %dynamic-slice_bitcast_fusion.4), channel_id=1, source_target_pairs={{0,2},{1,3},{2,0},{3,1},{4,6},{5,7},{6,4},{7,5},{8,10},{9,11},{10,... | collective-permute-start | bytes 2654216 | tf_op jit(solution)/shard_map/ppermute | solution.py:638
  382.9 46.5 %collective-permute-start.11 = (bf16[768,768]{1,0:T(8,128)(2,1)S(1)}, bf16[768,768]{1,0:T(8,128)(2,1)S(1)}, u32[]{:S(2)}, u32[]{:S(2)}) collective-permute-start(bf16[768,768]{1,0:T(8,128)(2,1)S(1)} %dynamic-slice_bitcast_fusion.2), channel_id=1, source_target_pairs={{0,2},{1,3},{2,0},{3,1},{4,6},{5,7},{6,4},{7,5},{8,10},{9,11},{10,... | collective-permute-start | bytes 3538952 | tf_op jit(solution)/shard_map/ppermute | solution.py:638
  386.9 66.9 %collective-permute-start.9 = (bf16[768,768]{1,0:T(8,128)(2,1)S(1)}, bf16[768,768]{1,0:T(8,128)(2,1)S(1)}, u32[]{:S(2)}, u32[]{:S(2)}) collective-permute-start(bf16[768,768]{1,0:T(8,128)(2,1)S(1)} %dynamic-slice_bitcast_fusion.3), channel_id=1, source_target_pairs={{0,2},{1,3},{2,0},{3,1},{4,6},{5,7},{6,4},{7,5},{8,10},{9,11},{10,... | collective-permute-start | bytes 3538952 | tf_op jit(solution)/shard_map/ppermute | solution.py:638
  (30 other events, 379.4 us)
Sparse Core Ops, SparseCore 0:
  373.0 33.7 all-reduce.5
  455.2 142.7 all-reduce.7

commit v3 on v2

--- a/solution.py
+++ b/solution.py
@@ -187,72 +187,6 @@
     return outs[0], outs[1], outs[2:]
 
 
-def return_kernel(sections, tensors, text, layout, text_out, layout_out, grad_out, layout_grad_out, send, recv):
-    section, t = lax.axis_index("section"), lax.axis_index("tensor")
-    length = text_out.shape[1]
-    greet(section, t, sections, tensors)
-    micro, page = t % 2, t // 2
-    kinds = ((grad_out, layout_grad_out), (text_out, layout_out))
-
-    def source(a, q):
-        start = q * length
-        return text.at[pl.ds(start, length)] if a == 0 else layout.at[:, pl.ds(start, length)]
-
-    def each(act):
-        for g in range(sections):
-            for q in range(tensors):
-                for a in range(2):
-                    @pl.when(section == g)
-                    def _():
-                        act(g, q, a, (micro == g) & (t == q))
-
-    def start(g, q, a, here):
-        src, dst = source(a, q), kinds[g][a].at[page]
-
-        @pl.when(here)
-        def _():
-            pltpu.make_async_copy(src, dst, recv.at[g, a, page]).start()
-
-        @pl.when(jnp.logical_not(here))
-        def _():
-            remote(src, dst, send.at[q, a], recv.at[g, a, page], {"section": micro, "tensor": q}).start()
-
-    def sent(g, q, a, here):
-        @pl.when(jnp.logical_not(here))
-        def _():
-            remote(
-                source(a, q), kinds[g][a].at[page], send.at[q, a], recv.at[g, a, page],
-                {"section": micro, "tensor": q},
-            ).wait_send()
-
-    each(start)
-    each(sent)
-    for g in range(sections):
-        for a in range(2):
-            for j in range(2):
-                dst = kinds[g][a].at[j]
-                remote(dst, dst, send.at[0, a], recv.at[g, a, j], {"tensor": (t + 1) % tensors}).wait_recv()
-
-
-def give_back(mesh, text, layout):
-    sections, tensors = mesh.shape["section"], mesh.shape["tensor"]
-    length = text.shape[0] // tensors
-    text_shape = jax.ShapeDtypeStruct((2, length, text.shape[1]), BF)
-    layout_shape = jax.ShapeDtypeStruct((2, layout.shape[0], length), BF)
-    return pl.pallas_call(
-        functools.partial(return_kernel, sections, tensors),
-        out_shape=(text_shape, layout_shape, text_shape, layout_shape),
-        in_specs=[ANY] * 2,
-        out_specs=[ANY] * 4,
-        scratch_shapes=[
-            pltpu.SemaphoreType.DMA((tensors, 2)),
-            pltpu.SemaphoreType.DMA((sections, 2, 2)),
-        ],
-        compiler_params=pltpu.CompilerParams(collective_id=1, has_side_effects=True),
-        name="give_back",
-    )(text, layout)
-
-
 GELU_P = 0.3275911
 GELU_A = (0.254829592, -0.284496736, 1.421413741, -1.453152027, 1.061405429)
 NN = (((1,), (0,)), ((), ()))
@@ -617,26 +551,339 @@
     return jax.tree.unflatten(out_tree, results[:-2]), tuple(results[-2:])
 
 
-def mm(spec, a, b):
-    return jnp.einsum(spec, a, b, preferred_element_type=F32)
-
-
 def zeros_like_tree(shapes):
     return jax.tree.map(lambda s: jnp.zeros(s.shape, s.dtype), shapes)
 
 
-def reduce_shard(grad, t, tensors):
-    sibling = [(i, i + 1 - 2 * (i % 2)) for i in range(tensors)]
-    partner = [(i, (i + tensors // 2) % tensors) for i in range(tensors)]
-    pairs = grad.reshape((2, tensors // 2) + grad.shape[1:])
+class Operands(typing.NamedTuple):
+    act: typing.Any
+    gf: typing.Any
+    low: typing.Any
+    dpre: typing.Any
+    x: typing.Any
+    dqkv: typing.Any
+    ctx: typing.Any
+    ga: typing.Any
+
+
+def gradient_rows(own):
+    return own.dqkv.shape[1], own.ctx.shape[1], own.low.shape[1], own.act.shape[2]
+
+
+def gradient_block(own, lowT, slot, which, first, rows):
+    if which == 0:
+        return dot(own.dqkv[slot, first : first + rows, :], own.x[...])
+    if which == 1:
+        return dot(own.ctx[slot, first : first + rows, :], own.ga[...])
+    if which == 2:
+        return dot(lowT[first : first + rows, :], own.dpre[slot])
+    return dot(own.act[slot, :, first : first + rows].T, own.gf[...])
+
+
+def chunks_of(own, step):
+    sizes = gradient_rows(own)
+    starts = [sum(sizes[:i]) for i in range(4)]
+    chunks = []
+    for which in (3, 2, 0, 1):
+        size = sizes[which]
+        piece = next(p for p in (step, 192, size) if size % p == 0)
+        chunks += [(starts[which] + f, piece, ((which, f, piece),)) for f in range(0, size, piece)]
+    return chunks
+
+
+def whole_chunk(own):
+    sizes = gradient_rows(own)
+    return (0, sum(sizes), tuple((which, 0, sizes[which]) for which in range(4)))
+
+
+def reduce_kernel(sections, tensors, chain, in_tree, *refs):
+    n_in = in_tree.num_leaves
+    hbm_in = refs[:n_in]
+    dx_t, dx_l, y_t, y_l, small_in = refs[n_in : n_in + 5]
+    results = refs[n_in + 5 : n_in + 7]
+    small_out, text_out, layout_out, grad_out, layout_grad_out = refs[n_in + 7 : n_in + 12]
+    rest = refs[n_in + 12 :]
+    operands = Staged(in_tree, hbm_in, rest[:n_in], rest[n_in], True)
+    lowT, raw, from_sibling, from_partner, near_in, cross_in, total = (
+        rest[n_in + 1 + 2 * i : n_in + 3 + 2 * i] for i in range(7)
+    )
+    small_got, small_sum, send, recv, out_sem, small_send, small_recv, page_send, page_recv = rest[n_in + 15 :]
+    section, d, t = lax.axis_index("section"), lax.axis_index("dp"), lax.axis_index("tensor")
     core, chip = t % 2, t // 2
-    theirs = lax.dynamic_index_in_dim(pairs, 1 - core, 1, keepdims=False)
-    mine = lax.dynamic_index_in_dim(pairs, core, 1, keepdims=False)
-    summed = (mine.astype(F32) + lax.ppermute(theirs, "tensor", sibling).astype(F32)).astype(BF)
-    theirs = lax.dynamic_index_in_dim(summed, 1 - chip, 0, keepdims=False)
-    mine = lax.dynamic_index_in_dim(summed, chip, 0, keepdims=False)
-    summed = (mine.astype(F32) + lax.ppermute(theirs, "tensor", partner).astype(F32)).astype(BF)
-    return lax.psum(summed, "dp").astype(F32)
+    sibling = {"tensor": t + 1 - 2 * core}
+    partner = {"tensor": (t + tensors // 2) % tensors}
+    near, cross = {"dp": d + 1 - 2 * (d % 2)}, {"dp": 3 - d}
+    outer = (d == 0) | (d == 3)
+    operands.start()
+    greet(section, t, sections, tensors, (near, cross) if chain else ())
+
+    length = text_out.shape[1]
+    micro, page = t % 2, t // 2
+    kinds = ((grad_out, layout_grad_out), (text_out, layout_out))
+    pages = ((dx_t, dx_l), (y_t, y_l))
+
+    def page_part(g, q, a):
+        return pages[g][a].at[pl.ds(q * length, length)] if a == 0 else pages[g][a].at[:, pl.ds(q * length, length)]
+
+    def each_page(act):
+        for g in range(sections):
+            for q in range(tensors):
+                for a in range(2):
+                    here = (micro == g) & (t == q)
+
+                    @pl.when((section == g) & here)
+                    def _():
+                        act(g, q, a, True)
+
+                    @pl.when((section == g) & jnp.logical_not(here))
+                    def _():
+                        act(g, q, a, False)
+
+    def page_copy(g, q, a):
+        return remote(
+            page_part(g, q, a), kinds[g][a].at[page], page_send.at[q, a], page_recv.at[g, a, page],
+            {"section": micro, "tensor": q},
+        )
+
+    def page_start(g, q, a, here):
+        if here:
+            pltpu.make_async_copy(page_part(g, q, a), kinds[g][a].at[page], page_recv.at[g, a, page]).start()
+        else:
+            page_copy(g, q, a).start()
+
+    def page_sent(g, q, a, here):
+        if not here:
+            page_copy(g, q, a).wait_send()
+
+    each_page(page_start)
+
+    def small_copy(i, device):
+        return remote(small_sum.at[i], small_got.at[i], small_send.at[i], small_recv.at[i], device)
+
+    small_sum[0] = small_in[...]
+    if chain:
+        small_copy(0, sibling).start()
+
+    own, own_in = operands.refs(), operands.parts()
+    work = [(1,) + whole_chunk(own[1])] + [(0,) + c for c in chunks_of(own[0], 256)]
+    for b in range(2):
+        wait(own_in[b].low)
+        lowT[b][...] = own[b].low[...].T
+    for b in (1, 0):
+        wait(*(part for part in own_in[b] if part is not own_in[b].low))
+
+    def span(ref, k):
+        return ref.at[pl.ds(work[k][1], work[k][2])]
+
+    def spans(ref, k):
+        return ref.at[:, pl.ds(work[k][1], work[k][2])]
+
+    def to_sibling(k):
+        b = work[k][0]
+        return remote(
+            spans(raw[b].at[1 - core], k), spans(from_sibling[b], k), send.at[0, k], recv.at[0, k], sibling
+        )
+
+    def to_partner(k):
+        b = work[k][0]
+        return remote(
+            span(raw[b].at[core, 1 - chip], k), span(from_partner[b], k), send.at[1, k], recv.at[1, k], partner
+        )
+
+    def to_near(k):
+        b = work[k][0]
+        return remote(span(raw[b].at[core, chip], k), span(near_in[b], k), send.at[2, k], recv.at[2, k], near)
+
+    def total_to_near(k):
+        b = work[k][0]
+        return remote(span(total[b], k), span(near_in[b], k), send.at[2, k], recv.at[2, k], near)
+
+    def to_cross(k):
+        b = work[k][0]
+        return remote(span(raw[b].at[core, chip], k), span(cross_in[b], k), send.at[3, k], recv.at[3, k], cross)
+
+    def out_copy(k, source):
+        b = work[k][0]
+        return pltpu.make_async_copy(span(source, k), span(results[b], k), out_sem.at[k])
+
+    def added(target, *sources):
+        target[...] = sum(s[...].astype(F32) for s in sources).astype(BF)
+
+    def stage_product(k):
+        b, first, rows, pieces = work[k]
+        for slot in range(tensors):
+            at = first
+            for which, begin, count in pieces:
+                raw[b][slot % 2, slot // 2, at : at + count, :] = gradient_block(
+                    own[b], lowT[b], slot, which, begin, count
+                ).astype(BF)
+                at += count
+        to_sibling(k).start()
+
+    def stage_sibling(k):
+        b = work[k][0]
+        to_sibling(k).wait_recv()
+        mine = raw[b].at[core, 1 - chip]
+        added(span(mine, k), span(mine, k), span(from_sibling[b].at[1 - chip], k))
+        to_partner(k).start()
+        mine = raw[b].at[core, chip]
+        added(span(mine, k), span(mine, k), span(from_sibling[b].at[chip], k))
+
+    def stage_partner(k):
+        b = work[k][0]
+        to_partner(k).wait_recv()
+        mine = span(raw[b].at[core, chip], k)
+        added(mine, mine, span(from_partner[b], k))
+        if not chain:
+            out_copy(k, raw[b].at[core, chip]).start()
+            return
+
+        @pl.when(outer)
+        def _():
+            to_near(k).start()
+
+    def stage_near(k):
+        b = work[k][0]
+
+        @pl.when(jnp.logical_not(outer))
+        def _():
+            to_near(k).wait_recv()
+            mine = span(raw[b].at[core, chip], k)
+            added(mine, mine, span(near_in[b], k))
+            to_cross(k).start()
+
+    def stage_cross(k):
+        b = work[k][0]
+
+        @pl.when(jnp.logical_not(outer))
+        def _():
+            to_cross(k).wait_recv()
+            added(span(total[b], k), span(raw[b].at[core, chip], k), span(cross_in[b], k))
+            total_to_near(k).start()
+            out_copy(k, total[b]).start()
+
+    def stage_total(k):
+        b = work[k][0]
+
+        @pl.when(outer)
+        def _():
+            to_near(k).wait_recv()
+            out_copy(k, near_in[b]).start()
+
+    stages = [stage_product, stage_sibling, stage_partner]
+    if chain:
+        stages += [stage_near, stage_cross, stage_total]
+    for step in range(len(work) + len(stages) - 1):
+        for lag, stage in enumerate(stages):
+            if 0 <= step - lag < len(work):
+                stage(step - lag)
+        if not chain:
+            continue
+        if step == 0:
+            small_copy(0, sibling).wait_recv()
+            small_sum[1] = small_sum[0] + small_got[0]
+            small_copy(1, partner).start()
+        if step == 1:
+            small_copy(1, partner).wait_recv()
+            small_sum[2] = small_sum[1] + small_got[1]
+            small_copy(2, near).start()
+        if step == 2:
+            small_copy(2, near).wait_recv()
+            small_sum[3] = small_sum[2] + small_got[2]
+
+            @pl.when(jnp.logical_not(outer))
+            def _():
+                small_copy(3, cross).start()
+
+        if step == 4:
+            @pl.when(jnp.logical_not(outer))
+            def _():
+                small_copy(3, cross).wait_recv()
+                small_sum[4] = small_sum[3] + small_got[3]
+                small_copy(4, near).start()
+
+        if step == 6:
+            @pl.when(outer)
+            def _():
+                small_copy(4, near).wait_recv()
+                small_sum[4] = small_got[4]
+
+            small_sum[5] = small_sum[4]
+            small_copy(5, {"section": 1 - section}).start()
+        if step == 8:
+            small_copy(5, {"section": 1 - section}).wait_recv()
+            small_out[0] = small_sum[5]
+            small_out[1] = small_got[5]
+
+    if chain:
+        for i, device in enumerate((sibling, partner, near)):
+            small_copy(i, device).wait_send()
+
+        @pl.when(jnp.logical_not(outer))
+        def _():
+            small_copy(3, cross).wait_send()
+            small_copy(4, near).wait_send()
+
+        small_copy(5, {"section": 1 - section}).wait_send()
+    else:
+        small_out[0] = small_in[...]
+        small_out[1] = small_in[...]
+    for k in range(len(work)):
+        to_sibling(k).wait_send()
+        to_partner(k).wait_send()
+        b = work[k][0]
+        if chain:
+            to_near(k).wait_send()
+
+            @pl.when(jnp.logical_not(outer))
+            def _():
+                to_cross(k).wait_send()
+
+        out_copy(k, total[b]).wait()
+    each_page(page_sent)
+    for g in range(sections):
+        for a in range(2):
+            for j in range(2):
+                dst = kinds[g][a].at[j]
+                remote(dst, dst, page_send.at[0, a], page_recv.at[g, a, j], partner).wait_recv()
+
+
+def reduce_all(mesh, operands, dx, y, small):
+    sections, dp, tensors = mesh.shape["section"], mesh.shape["dp"], mesh.shape["tensor"]
+    chain = dp == 4
+    flat_in, in_tree = jax.tree.flatten(operands)
+    length = dx[0].shape[0] // tensors
+    rows = [sum(gradient_rows(own)) for own in operands]
+    widths = [own.x.shape[1] for own in operands]
+    n_chunks = 1 + len(chunks_of(operands[0], 256))
+    text_shape, layout_shape = shape((2, length, widths[0])), shape((2, widths[1], length))
+    big = [pltpu.VMEM((r, w), BF) for r, w in zip(rows, widths)]
+    scratch = [pltpu.VMEM(x.shape, x.dtype) for x in flat_in] + [pltpu.SemaphoreType.DMA((len(flat_in),))]
+    scratch += [pltpu.VMEM((own.low.shape[1], own.low.shape[0]), BF) for own in operands]
+    scratch += [pltpu.VMEM((2, tensors // 2, r, w), BF) for r, w in zip(rows, widths)]
+    scratch += [pltpu.VMEM((tensors // 2, r, w), BF) for r, w in zip(rows, widths)]
+    scratch += big * 4
+    scratch += [pltpu.VMEM((6,) + small.shape, F32)] * 2
+    scratch += [pltpu.SemaphoreType.DMA((4, n_chunks))] * 2 + [pltpu.SemaphoreType.DMA((n_chunks,))]
+    scratch += [pltpu.SemaphoreType.DMA((6,))] * 2
+    scratch += [pltpu.SemaphoreType.DMA((tensors, 2)), pltpu.SemaphoreType.DMA((sections, 2, 2))]
+    total_t, total_l, small, *pages = pl.pallas_call(
+        functools.partial(reduce_kernel, sections, tensors, chain, in_tree),
+        out_shape=[shape((r, w)) for r, w in zip(rows, widths)]
+        + [shape((2,) + small.shape, F32), text_shape, layout_shape, text_shape, layout_shape],
+        in_specs=[ANY] * (len(flat_in) + 4) + [VMEM],
+        out_specs=[ANY] * 2 + [VMEM] + [ANY] * 4,
+        scratch_shapes=scratch,
+        compiler_params=pltpu.CompilerParams(
+            collective_id=1, has_side_effects=True, vmem_limit_bytes=62 << 20
+        ),
+        name="reduce_all",
+    )(*flat_in, dx[0], dx[1].T, y[0], y[1].T, small)
+    if not chain:
+        total_t, total_l = lax.psum((total_t, total_l), "dp")
+        both = lax.psum(small[0], ("dp", "tensor"))
+        small = jnp.stack([both, lax.ppermute(both, "section", [(0, 1), (1, 0)])])
+    return (total_t, total_l), small, pages
 
 
 def per_device(
@@ -707,41 +954,37 @@
         section == 0, lambda old, got: back(got), lambda old, got: old, first, hopped
     )
     downs = tuple(res.dx for res in back_results)
-    grads = [
-        (
-            mm("tnl,ld->tnd", res.dqkv, rows[b]).astype(BF),
-            mm("tnl,ld->tnd", saved[1][b].ctx, res.ga).astype(BF),
-            mm("ld,tln->tdn", saved[1][b].low, res.dpre).astype(BF),
-            mm("tln,ld->tnd", saved[1][b].act, res.gf).astype(BF),
-        )
-        for b, res in enumerate(back_results)
-    ]
-    final = tuple(jnp.where(section == 0, d, o) for d, o in zip(downs, outs))
-    text_out, layout_out, text_grad, layout_grad = give_back(mesh, final[0], final[1].T)
-    summed = [[reduce_shard(g, t, tensors) for g in per_stream] for per_stream in grads]
-
+    operands = tuple(
+        Operands(act=k.act, gf=res.gf, low=k.low, dpre=res.dpre, x=x, dqkv=res.dqkv, ctx=k.ctx, ga=res.ga)
+        for x, k, res in zip(rows, saved[1], back_results)
+    )
     own_group = lax.dynamic_index_in_dim(lang_ids[:, page], micro, 0, keepdims=False)
     page_sum = jnp.where(section == 0, jnp.sum(downs[0].astype(F32), axis=0), 0.0)
     lang_grad = (groups == own_group).astype(F32)[:, None] * page_sum[None, :]
-    pick = (jnp.arange(2, dtype=jnp.int32) == section).astype(F32)[:, None, None]
-    small = lax.psum(
-        tuple(pick * member[None] for sums in norm_grads for member in (sums[0:2], sums[2:4])) + (lang_grad,),
-        ("section", "dp", "tensor"),
+    wide = text_gains.shape[-1]
+    small = jnp.concatenate(
+        [lang_grad, norm_grads[0], jnp.pad(norm_grads[1], ((0, 0), (0, wide - norm_grads[1].shape[1])))]
     )
-
-    def own_row(stacked):
-        return lax.dynamic_slice_in_dim(stacked, section, 1, 0)
+    totals, small, (text_out, layout_out, text_grad, layout_grad) = reduce_all(mesh, operands, downs, outs, small)
+    n_lang = lang_table.shape[0]
+    lang_sum = jnp.where(section == 0, small[0, :n_lang], small[1, :n_lang])
+    norm_sums = (small[0, n_lang : n_lang + 4], small[0, n_lang + 4 : n_lang + 8, : layout_gains.shape[-1]])
+    summed = []
+    for total, own in zip(totals, operands):
+        sizes = gradient_rows(own)
+        starts = [sum(sizes[:i]) for i in range(4)]
+        summed.append([total[s : s + n].astype(F32) for s, n in zip(starts, sizes)])
 
     def unflat(grad, like):
         return jnp.transpose(grad.reshape(like.shape[2], like.shape[3], like.shape[1]), (2, 0, 1))[None]
 
     unflip = lambda block: jnp.transpose(block, (0, 2, 1))[None]
     return (
-        text_out[None], unflip(layout_out), text_grad[None], unflip(layout_grad), small[4],
+        text_out[None], unflip(layout_out), text_grad[None], unflip(layout_grad), lang_sum,
         unflat(summed[0][0], text_project), summed[0][1][None], summed[0][2][None], summed[0][3][None],
-        own_row(small[0]), own_row(small[1]),
+        norm_sums[0][None, 0:2], norm_sums[0][None, 2:4],
         unflat(summed[1][0], layout_project), summed[1][1][None], summed[1][2][None], summed[1][3][None],
-        own_row(small[2]), own_row(small[3]),
+        norm_sums[1][None, 0:2], norm_sums[1][None, 2:4],
     )
 
 

time: 626 us -> 471 us (0.75)
  waiting for transfers between devices: 232 us -> 86.2 us
  Pallas kernels: 206 us -> 321 us
  blocking collectives: 46.8 us -> 0 us
  other arithmetic: 38.3 us -> 17.2 us
  matrix products: 20.4 us -> 0.2 us
  between operations: 15.1 us -> 1.33 us
  local copies, waits for them, and re-layouts: 39.4 us -> 28.2 us
  starting transfers between devices: 17.3 us -> 6.74 us
    pallas_call x1, Pallas kernels: 12.6 us -> 130 us  [reduce_all(): pl.pallas_call(functools.partial(reduce_kernel, sections, tensors, chain,...]
    psum x2 -> x0, waiting for transfers between devices: 75.3 us -> none  [reduce_shard(): return lax.psum(summed, 'dp').astype(F32)]
    ppermute x16 -> x0, waiting for transfers between devices: 63.1 us -> none  [the longest x8 63 us: reduce_shard(): lax.ppermute(theirs, 'tensor', partner).astype(F32)]
    psum x1 -> x0, blocking collectives: 46.8 us -> none  [per_device(): lax.psum(tuple((pick * member[None] for sums in norm_grads for member in...]
    dot_general x8 -> x0, matrix products: 20.2 us -> none  [mm(): return jnp.einsum(spec, a, b, preferred_element_type=F32)]
    convert_element_type x11 -> x0, other arithmetic: 14.6 us -> none  [the longest x8 12.8 us: reduce_shard(): (mine.astype(F32) + lax.ppermute(theirs, 'tensor', sibling).astype(F32))....]
    ppermute x16 -> x0, starting transfers between devices: 10.2 us -> none  [the longest x8 8.52 us: reduce_shard(): lax.ppermute(theirs, 'tensor', partner).astype(F32)]
    dynamic_slice x6 -> x0, local copies, waits for them, and re-layouts: 6.86 us -> none  [the longest x2 3.25 us: reduce_shard(): theirs = lax.dynamic_index_in_dim(pairs, 1 - core, 1, keepdims=False)]
  transfers between devices with their start and end apart: 22 -> 4, of which waited for: 7 -> 2; matrix products, arithmetic and copies ran while one was open for 10% -> 1% of each run, Pallas kernels for 2% -> 0%
where the time goes in v3:
time: 471 us; the launch traced here: 462 us
  Pallas kernels  321 us (68%)
  waiting for transfers between devices  86.2 us (18%)
  local copies, waits for them, and re-layouts  28.2 us (6%)
  other arithmetic  17.2 us (4%)
  starting transfers between devices  6.74 us (1%)
    pallas_call x1, Pallas kernels, reduce_all(): pl.pallas_call(functools.partial(reduce_kernel, sections, tensors, chain,...  130 us
    pallas_call x1, Pallas kernels, fetch(): pl.pallas_call(functools.partial(fetch_kernel, sections, tensors, dp, sha...  127 us
    ppermute x2, waiting for transfers between devices, per_device(): lax.ppermute(res.dx, 'section', [(1, 0)])  73.1 us
    pallas_call x1, Pallas kernels, layer_backward(): pl.pallas_call(functools.partial(backward_kernel, in_tree, out_tree), out...  32.5 us
    pallas_call x1, Pallas kernels, layer_forward(): pl.pallas_call(functools.partial(forward_kernel, in_tree, out_tree), out_...  31.1 us
    ppermute x2, waiting for transfers between devices, per_device(): lax.ppermute(block, 'section', [(0, 1)])  13 us
    another operation x13, local copies, waits for them, and re-layouts  12.2 us
  transfers between devices with their start and end apart: 4, of which 2 were waited for; matrix products, arithmetic and copies ran while one was open for 1% of the time, Pallas kernels for 0%

profile of v3, /device:TPU:0, one launch (start us, length us, event | category | flops | bytes accessed | tf_op | source)
XLA Modules:
  0.0 461.8 jit_solution(17640767980863792418)
XLA Ops:
  4.2 1.8 fusion.refs_0_
  6.1 127.4 %fetch.1 = (bf16[512,768]{1,0:T(8,128)(2,1)}, bf16[192,512]{1,0:T(8,128)(2,1)}, bf16[4,576,768]{2,1,0:T(8,128)(2,1)}, bf16[4,192,768]{2,1,0:T(8,128)(2,1)}, bf16...) custom-call(bf16[2,128,768]{2,1,0:T(8,128)(2,1)} %fusion.refs_0_, ...), custom_call_target="tpu_custom_call" | custom-call | tf_op jit(solution)/shard_map/fetch/pallas_call | solution.py:172
  133.5 35.6 %conditional.4 = (bf16[512,768]{1,0:T(8,128)(2,1)}, bf16[512,192]{1,0:T(8,128)(2,1)}, bf16[512,768]{1,0:T(8,128)(2,1)}, bf16[512,192]{1,0:T(8,128)(2,1)}, bf16[4...) conditional(s32[]{:T(128)} %convert_element_type.44, () %tuple.47, ...), branch_computations={%region_0.1_spmd, %region_1.2_spmd} | conditional | flops 512 | bytes 24977654 | solution.py:943
  134.1 1.8 copy.37.refs_1_
  135.8 2.1 copy.64
  137.9 31.1 %layer_forward.2 = (bf16[512,768]{1,0:T(8,128)(2,1)}, bf16[512,192]{1,0:T(8,128)(2,1)}, bf16[4,3,512,512]{3,2,1,0:T(8,128)(2,1)}, bf16[4,576,512]{2,1,0:T(8,128)...) custom-call(bf16[512,768]{1,0:T(8,128)(2,1)} %get-tuple-element.669., ...), custom_call_target="tpu_custom_call" | custom-call | tf_op jit(solution)/shard_map/cond/branch_1_fun/layer_forward/pallas_call | solution.py:419
  169.1 2.2 collective-permute-start
  171.2 2.0 collective-permute-start.1
  173.2 13.0 %collective-permute-done.1 = bf16[512,192]{1,0:T(8,128)(2,1)} collective-permute-done((bf16[512,192]{1,0:T(8,128)(2,1)}, bf16[512,192]{1,0:T(8,128)(2,1)}, u32[]{:S(2)}, u32[]{:S(2)}) %collective-permute-start.1) | collective-permute-done | bytes 196640 | tf_op jit(solution)/shard_map/ppermute | solution.py:944
  186.4 10.9 %conditional.6 = ((bf16[512,768]{1,0:T(8,128)(2,1)}, bf16[4,576,512]{2,1,0:T(8,128)(2,1)}, bf16[512,768]{1,0:T(8,128)(2,1)}, bf16[4,512,768]{2,1,0:T(8,128)(2,1)...) conditional(s32[]{:T(128)} %convert_element_type.43, () %tuple.50, ...), branch_computations={%region_4.5_spmd, %region_5.6_spmd} | conditional | bytes 9845892 | solution.py:951
  193.4 1.6 broadcast.72
  195.0 1.9 broadcast.73
  201.2 1.8 copy.40
  202.9 73.1 %collective-permute-done.3 = bf16[512,192]{1,0:T(8,128)(2,1)} collective-permute-done((bf16[512,192]{1,0:T(8,128)(2,1)}, bf16[512,192]{1,0:T(8,128)(2,1)}, u32[]{:S(2)}, u32[]{:S(2)}) %collective-permute-start.3) | collective-permute-done | bytes 196640 | tf_op jit(solution)/shard_map/ppermute | solution.py:952
  276.1 32.7 %conditional.7 = (bf16[512,768]{1,0:T(8,128)(2,1)}, bf16[4,576,512]{2,1,0:T(8,128)(2,1)}, bf16[512,768]{1,0:T(8,128)(2,1)}, bf16[4,512,768]{2,1,0:T(8,128)(2,1)}...) conditional(s32[]{:T(128)} %convert_element_type.44, ...), branch_computations={%region_6.7_spmd, %region_7.8_spmd} | conditional | bytes 112 | solution.py:953
  276.2 32.5 %layer_backward.4 = (bf16[512,768]{1,0:T(8,128)(2,1)}, bf16[4,576,512]{2,1,0:T(8,128)(2,1)}, bf16[512,768]{1,0:T(8,128)(2,1)}, bf16[4,512,768]{2,1,0:T(8,128)(2,...) custom-call(bf16[512,768]{1,0:T(8,128)(2,1)} %get-tuple-element.430., ...), custom_call_target="tpu_custom_call" | custom-call | tf_op jit(solution)/shard_map/cond/branch_1_fun/layer_backward/pallas_call | solution.py:539
  310.1 1.8 copy.39
  312.5 130.2 %reduce_all.1 = (bf16[2304,768]{1,0:T(8,128)(2,1)}, bf16[576,192]{1,0:T(8,128)(2,1)}, f32[2,16,768]{2,1,0:T(8,128)}, bf16[2,128,768]{2,1,0:T(8,128)(2,1)}, bf16[...) custom-call(bf16[4,512,768]{2,1,0:T(8,128)(2,1)} %get-tuple-element.553.refs_0_, ...), custom_call_target="tpu_custom_call" | custom-call | tf_op jit(solution)/shard_map/reduce_all/pallas_call | solution.py:870
  442.7 1.5 fusion.7
  444.2 1.4 fusion.8
  445.6 1.4 select_bitcast_fusion
  449.2 1.7 bitcast_convert_fusion.3
  450.9 1.8 bitcast_convert_fusion.2
  454.0 2.5 bitcast_convert_fusion
  (60 shorter events, 25.4 us)
Async XLA Ops:
  0.7 3.4 copy-start
  6.0 127.4 %copy-start.6 = (f32[1,2,768]{2,1,0:T(2,128)S(1)}, f32[1,2,768]{2,1,0:T(2,128)}, u32[]{:S(2)}) copy-start(f32[1,2,768]{2,1,0:T(2,128)} %param.40) | copy-start | bytes 18436
  6.0 127.4 %copy-start.9 = (f32[1,2,192]{2,1,0:T(2,128)S(1)}, f32[1,2,192]{2,1,0:T(2,128)}, u32[]{:S(2)}) copy-start(f32[1,2,192]{2,1,0:T(2,128)} %param.46) | copy-start | bytes 4612
  6.0 127.4 %copy-start.10 = (f32[1,2,768]{2,1,0:T(2,128)S(1)}, f32[1,2,768]{2,1,0:T(2,128)}, u32[]{:S(2)}) copy-start(f32[1,2,768]{2,1,0:T(2,128)} %param.41) | copy-start | bytes 18436
  6.0 127.4 %copy-start.11 = (f32[1,2,192]{2,1,0:T(2,128)S(1)}, f32[1,2,192]{2,1,0:T(2,128)}, u32[]{:S(2)}) copy-start(f32[1,2,192]{2,1,0:T(2,128)} %param.47) | copy-start | bytes 4612
  169.1 17.2 %collective-permute-start = (bf16[512,768]{1,0:T(8,128)(2,1)}, bf16[512,768]{1,0:T(8,128)(2,1)}, u32[]{:S(2)}, u32[]{:S(2)}) collective-permute-start(bf16[512,768]{1,0:T(8,128)(2,1)} %get-tuple-element.551), channel_id=1, source_target_pairs={{0,16},{1,17},{2,18},{3,19},{4,20},{5,21},{6,22},{7,23},{8,24},{9,... | collective-permute-start | bytes 2359304 | tf_op jit(solution)/shard_map/ppermute | solution.py:944
  171.2 15.0 %collective-permute-start.1 = (bf16[512,192]{1,0:T(8,128)(2,1)}, bf16[512,192]{1,0:T(8,128)(2,1)}, u32[]{:S(2)}, u32[]{:S(2)}) collective-permute-start(bf16[512,192]{1,0:T(8,128)(2,1)} %get-tuple-element.552), channel_id=1, source_target_pairs={{0,16},{1,17},{2,18},{3,19},{4,20},{5,21},{6,22},{7,23},{8,24},{9,... | collective-permute-start | bytes 589832 | tf_op jit(solution)/shard_map/ppermute | solution.py:944
  186.4 13.5 %copy-start.12 = (s32[2,2]{1,0:T(2,128)S(1)}, s32[2,2]{1,0:T(2,128)}, u32[]{:S(2)}) copy-start(s32[2,2]{1,0:T(2,128)} %param.34) | copy-start | bytes 52
  197.3 78.8 %collective-permute-start.2 = (bf16[512,768]{1,0:T(8,128)(2,1)}, bf16[512,768]{1,0:T(8,128)(2,1)}, u32[]{:S(2)}, u32[]{:S(2)}) collective-permute-start(bf16[512,768]{1,0:T(8,128)(2,1)} %get-tuple-element.567), channel_id=1, source_target_pairs={{16,0},{17,1},{18,2},{19,3},{20,4},{21,5},{22,6},{23,7},{24,8},{25... | collective-permute-start | bytes 2359304 | tf_op jit(solution)/shard_map/ppermute | solution.py:952
  198.6 77.4 %collective-permute-start.3 = (bf16[512,192]{1,0:T(8,128)(2,1)}, bf16[512,192]{1,0:T(8,128)(2,1)}, u32[]{:S(2)}, u32[]{:S(2)}) collective-permute-start(bf16[512,192]{1,0:T(8,128)(2,1)} %get-tuple-element.568), channel_id=1, source_target_pairs={{16,0},{17,1},{18,2},{19,3},{20,4},{21,5},{22,6},{23,7},{24,8},{25... | collective-permute-start | bytes 589832 | tf_op jit(solution)/shard_map/ppermute | solution.py:952
  442.7 11.2 %copy-start.3 = (bf16[2304,768]{1,0:T(8,128)(2,1)S(1)}, bf16[2304,768]{1,0:T(8,128)(2,1)}, u32[]{:S(2)}) copy-start(bf16[2304,768]{1,0:T(8,128)(2,1)} %get-tuple-element.596) | copy-start | bytes 10616836
  456.5 2.0 copy-start.5
  456.5 2.8 copy-start.8
  456.5 3.4 copy-start.4
  456.5 4.2 copy-start.7
  456.5 4.8 %copy-start.1 = (f32[8,768]{1,0:T(8,128)S(1)}, f32[8,768]{1,0:T(8,128)}, u32[]{:S(2)}) copy-start(f32[8,768]{1,0:T(8,128)} %param.35) | copy-start | bytes 73732
